TPU v7x, 512 devices: a whole 4x8x8 slice. The times are simulated.
512 devices in a mesh: subj: 16 (over y_lo, x), depth: 32 (over y_hi, z, core).
Axes of the slice: x: 4, y: 8 (y_hi: 2, y_lo: 4; y = y_hi * 4 + y_lo), z: 8, core: 2. Of those that a mesh axis runs over, the one named last changes fastest.
Arguments:
- images: float32 [16, 160, 128, 128], P('subj', 'depth'), may hold values from -6 to 6
- velocity: float32 [3, 16, 160, 128, 128], P(None, 'subj', 'depth'), may hold values from -3 to 3
- ref_index: int32 [4], replicated, may hold values from 0 to 15
- ref_weights: int32 [16, 4], P('subj'), may hold values from 0 to 16
Outputs:
- velocity_out: float32 [3, 16, 160, 128, 128], P(None, 'subj', 'depth')
Inputs may be any that keep to these rules, and one draw needn't show every extreme that they name: `ref_index`: subject indices of the references; they may repeat. `ref_weights`: numerators over 16.
All inputs are finite; a program needn't handle non-finite values.
Results may differ from a plain program's by a relative error of at most 0.0003.
Values sent between devices are 32-bit elements; how exact they have to be, the bound alone decides.
A program may use at most 64 MiB of HBM per device.

v0:
```python
import math

import jax
import jax.numpy as jnp
from jax import lax
from jax.sharding import PartitionSpec as P

X = 128
Y = 128
ZD = 5
SUBJ_DEV = 1
NREF = 4
WIN = 9
RG = 3
WDEN = 16


def padded(shard, sides, width):
    for axis, dim in sides:
        devices, length = (lax.axis_size(axis), shard.shape[dim])
        up = [(i, (i + 1) % devices) for i in range(devices - 1)]
        down = [(j, i) for i, j in up]
        last = lax.slice_in_dim(shard, length - width, length, axis=dim)
        first = lax.slice_in_dim(shard, 0, width, axis=dim)
        before = lax.ppermute(last, axis, up)
        after = lax.ppermute(first, axis, down)
        shard = jnp.concatenate([before, shard, after], axis=dim)
    return shard


def spread(shard, axis, root):
    mine = lax.axis_index(axis) == root
    return lax.psum(jnp.where(mine, shard, jnp.zeros_like(shard)), axis)


def gauss_taps():
    raw = [math.exp(-0.5 * offset * offset) for offset in range(-RG, RG + 1)]
    total = sum(raw)
    return [value / total for value in raw]


def band_matrix(length, taps):
    radius = len(taps) // 2
    rows_idx = lax.broadcasted_iota(jnp.int32, (length, length), 0)
    cols_idx = lax.broadcasted_iota(jnp.int32, (length, length), 1)
    matrix = jnp.zeros((length, length), jnp.float32)
    for offset in range(len(taps)):
        matrix = matrix + jnp.where(rows_idx - cols_idx == offset - radius, taps[offset], 0.0)
    return matrix


def planes_xy(field, matrix_x, matrix_y):
    across = jnp.dot(field, matrix_y, precision=lax.Precision.HIGHEST)
    return jnp.einsum("wx,pxy->pwy", matrix_x, across, precision=lax.Precision.HIGHEST)


def depth_window(field, taps, planes, axis):
    total = taps[0] * lax.slice_in_dim(field, 0, planes, axis=axis)
    for offset in range(1, len(taps)):
        total = total + taps[offset] * lax.slice_in_dim(field, offset, offset + planes, axis=axis)
    return total


def boxed(field, box_x, box_y):
    summed = depth_window(field, [1.0] * WIN, ZD, 0)
    return planes_xy(summed, box_x, box_y) / float(WIN**3)


def local_slab(images, which):
    slot_idx = which % SUBJ_DEV
    return lax.dynamic_index_in_dim(images, slot_idx, 0, keepdims=False)


def on_device(images, velocity, ref_index, ref_weights):
    radius = WIN // 2
    ones_taps = [1.0] * WIN
    box_x = band_matrix(X, ones_taps)
    box_y = band_matrix(Y, ones_taps)
    taps = gauss_taps()
    smooth_x = band_matrix(X, taps)
    smooth_y = band_matrix(Y, taps)
    own_ext = padded(images, (("depth", 1),), radius + 1)
    sent = []
    for refnum in range(NREF):
        which = ref_index[refnum]
        sent.append(spread(local_slab(images, which), "subj", which // SUBJ_DEV))
    ref_ext = padded(jnp.stack(sent), (("depth", 1),), radius)
    moving_ext = own_ext[0]
    inner = moving_ext[1:-1]
    core = moving_ext[radius + 1 : radius + 1 + ZD]
    mean_i = boxed(inner, box_x, box_y)
    var_i = boxed(inner * inner, box_x, box_y) - mean_i * mean_i + 1e-05
    coeffs = jnp.zeros_like(core)
    for refnum in range(NREF):
        fixed_ext = ref_ext[refnum]
        fixed_core = fixed_ext[radius : radius + ZD]
        mean_j = boxed(fixed_ext, box_x, box_y)
        var_j = boxed(fixed_ext * fixed_ext, box_x, box_y) - mean_j * mean_j + 1e-05
        covariance = boxed(inner * fixed_ext, box_x, box_y) - mean_i * mean_j
        term = (
            2.0
            * covariance
            / (var_i * var_j)
            * (fixed_core - mean_j - covariance / var_i * (core - mean_i))
        )
        coeffs = coeffs + ref_weights[0, refnum].astype(jnp.float32) / float(WDEN) * term
    grad_depth = (moving_ext[radius + 2 : radius + 2 + ZD] - moving_ext[radius : radius + ZD]) * 0.5
    pad_x = jnp.pad(core, ((0, 0), (1, 1), (0, 0)))
    grad_x = (pad_x[:, 2:, :] - pad_x[:, :-2, :]) * 0.5
    pad_y = jnp.pad(core, ((0, 0), (0, 0), (1, 1)))
    grad_y = (pad_y[:, :, 2:] - pad_y[:, :, :-2]) * 0.5
    forces = [jnp.stack([coeffs * grad_depth, coeffs * grad_x, coeffs * grad_y])]
    force_all = jnp.stack(forces, axis=1)
    force_ext = padded(force_all, (("depth", 2),), RG)
    summed = depth_window(force_ext, taps, ZD, 2)
    flat = summed.reshape((3 * SUBJ_DEV * ZD, X, Y))
    smooth = planes_xy(flat, smooth_x, smooth_y).reshape((3, SUBJ_DEV, ZD, X, Y))
    return velocity + 40.0 * smooth


def solution(mesh):
    placed = (
        P("subj", "depth", None, None),
        P(None, "subj", "depth", None, None),
        P(),
        P("subj", None),
    )
    return jax.shard_map(
        on_device,
        mesh=mesh,
        in_specs=placed,
        out_specs=P(None, "subj", "depth", None, None),
        check_vma=False,
    )
```

profile of v0, /device:TPU:48, one launch (start us, length us, event | category | flops | bytes accessed | tf_op | source)
XLA Modules:
  0.0 281.9 jit_solution(16324112334780596169)
XLA Ops:
  6.5 1.1 copy.5
  7.7 11.7 %collective-permute-start.1 = (f32[1,5,128,128]{2,3,1,0:T(8,128)S(1)}, f32[1,5,128,128]{2,3,1,0:T(8,128)S(1)}, u32[]{:S(2)}, u32[]{:S(2)}) collective-permute-start(f32[1,5,128,128]{2,3,1,0:T(8,128)S(1)} %copy.5), channel_id=1, source_target_pairs={{1,0},{2,1},{3,2},{4,3},{5,4},{6,5},{7,6},{8,7},{9,8},{10,9},{11,1... | collective-permute-start | bytes 983048 | tf_op jit(solution)/shard_map/ppermute | solution.py:26
  19.4 1.9 collective-permute-start
  21.3 1.5 fusion.573
  25.3 1.9 collective-permute-done.1
  27.3 9.8 %collective-permute-done = f32[1,5,128,128]{2,3,1,0:T(8,128)S(1)} collective-permute-done((f32[1,5,128,128]{2,3,1,0:T(8,128)S(1)}, f32[1,5,128,128]{2,3,1,0:T(8,128)S(1)}, u32[]{:S(2)}, u32[]{:S(2)}) %collective-permute-start) | collective-permute-done | bytes 327712 | tf_op jit(solution)/shard_map/ppermute | solution.py:25
  37.7 1.5 bitcast_subtract_fusion
  39.2 155.9 %all-reduce.5.cloned.1.call-done = (f32[5,128,128]{1,2,0:T(8,128)}, f32[5,128,128]{1,2,0:T(8,128)}, f32[5,128,128]{1,2,0:T(8,128)}, f32[5,128,128]{1,2,0:T(8,128)}) async-done(((f32[5,128,128]{1,2,0:T(8,128)}, f32[5,128,128]{1,2,0:T(8,128)}, f32[5,128,128]{1,2,0:T(8,128)}, f32[5,128,128]{1,2,0:T(8,128)}), (f32[5,128,128]{1,2,0:T(8,128)}, f32[5,128,128]{1,2,0:T(8,128)}, f32[5,128,128]{1,2,0:T(8,128)}, ...) | async-done | bytes 1310736 | tf_op jit(solution)/shard_map/psum | solution.py:33
  195.1 1.4 pad_maximum_fusion.2
  196.7 1.9 collective-permute-start.2
  198.7 9.7 %collective-permute-start.3 = (f32[4,4,128,128]{2,3,1,0:T(8,128)S(1)}, f32[4,4,128,128]{2,3,1,0:T(8,128)S(1)}, u32[]{:S(2)}, u32[]{:S(2)}) collective-permute-start(f32[4,4,128,128]{2,3,1,0:T(8,128)S(1)} %get-tuple-element.19), channel_id=1, source_target_pairs={{1,0},{2,1},{3,2},{4,3},{5,4},{6,5},{7,6},{8,7},{9,8},{10,9},{11,1... | collective-permute-start | bytes 3145736 | tf_op jit(solution)/shard_map/ppermute | solution.py:26
  208.3 0.7 fusion.572
  212.8 17.3 %collective-permute-done.2 = f32[4,4,128,128]{2,3,1,0:T(8,128)S(1)} collective-permute-done((f32[4,4,128,128]{2,3,1,0:T(8,128)S(1)}, f32[4,4,128,128]{2,3,1,0:T(8,128)S(1)}, u32[]{:S(2)}, u32[]{:S(2)}) %collective-permute-start.2) | collective-permute-done | bytes 1048608 | tf_op jit(solution)/shard_map/ppermute | solution.py:25
  230.1 1.8 collective-permute-done.3
  235.9 1.0 slice_multiply_fusion.7
  245.3 0.9 fusion.46
  246.8 0.8 fusion.567
  247.8 1.9 collective-permute-start.4
  249.7 9.8 %collective-permute-start.5 = (f32[3,1,3,128,128]{3,4,2,1,0:T(8,128)S(1)}, f32[3,1,3,128,128]{3,4,2,1,0:T(8,128)S(1)}, u32[]{:S(2)}, u32[]{:S(2)}) collective-permute-start(f32[3,1,3,128,128]{3,4,2,1,0:T(8,128)S(1)} %get-tuple-element.21), channel_id=1, source_target_pairs={{1,0},{2,1},{3,2},{4,3},{5,4},{6,5},{7,6},{8,7},{9,8},{10,9},{11,1... | collective-permute-start | bytes 1769480 | tf_op jit(solution)/shard_map/ppermute | solution.py:26
  259.6 9.9 %collective-permute-done.4 = f32[3,1,3,128,128]{3,4,2,1,0:T(8,128)S(1)} collective-permute-done((f32[3,1,3,128,128]{3,4,2,1,0:T(8,128)S(1)}, f32[3,1,3,128,128]{3,4,2,1,0:T(8,128)S(1)}, u32[]{:S(2)}, u32[]{:S(2)}) %collective-permute-start.4) | collective-permute-done | bytes 589856 | tf_op jit(solution)/shard_map/ppermute | solution.py:25
  269.4 1.8 collective-permute-done.5
  271.6 1.0 fusion.191
  272.7 1.0 convolution_multiply_fusion
  274.0 1.1 add.1130
  (48 shorter events, 15.8 us)
Async XLA Ops:
  6.5 188.6 %all-reduce.5.cloned.1.call-start = ((), (), s32[]{:S(2)}) async-start(), calls=%async_computation | async-start | bytes 2621440 | tf_op jit(solution)/shard_map/psum | solution.py:33
  7.7 19.6 %collective-permute-start.1 = (f32[1,5,128,128]{2,3,1,0:T(8,128)S(1)}, f32[1,5,128,128]{2,3,1,0:T(8,128)S(1)}, u32[]{:S(2)}, u32[]{:S(2)}) collective-permute-start(f32[1,5,128,128]{2,3,1,0:T(8,128)S(1)} %copy.5), channel_id=1, source_target_pairs={{1,0},{2,1},{3,2},{4,3},{5,4},{6,5},{7,6},{8,7},{9,8},{10,9},{11,1... | collective-permute-start | bytes 983048 | tf_op jit(solution)/shard_map/ppermute | solution.py:26
  19.4 17.7 %collective-permute-start = (f32[1,5,128,128]{2,3,1,0:T(8,128)S(1)}, f32[1,5,128,128]{2,3,1,0:T(8,128)S(1)}, u32[]{:S(2)}, u32[]{:S(2)}) collective-permute-start(f32[1,5,128,128]{2,3,1,0:T(8,128)S(1)} %copy.5), channel_id=1, source_target_pairs={{0,1},{1,2},{2,3},{3,4},{4,5},{5,6},{6,7},{7,8},{8,9},{9,10},{10,1... | collective-permute-start | bytes 983048 | tf_op jit(solution)/shard_map/ppermute | solution.py:25
  196.5 11.8 %copy-start.5 = (s32[1,4]{1,0:T(1,128)S(1)}, s32[1,4]{1,0:T(1,128)}, u32[]{:S(2)}) copy-start(s32[1,4]{1,0:T(1,128)} %param.7) | copy-start | bytes 52
  196.7 33.4 %collective-permute-start.2 = (f32[4,4,128,128]{2,3,1,0:T(8,128)S(1)}, f32[4,4,128,128]{2,3,1,0:T(8,128)S(1)}, u32[]{:S(2)}, u32[]{:S(2)}) collective-permute-start(f32[4,4,128,128]{2,3,1,0:T(8,128)S(1)} %get-tuple-element.18), channel_id=1, source_target_pairs={{0,1},{1,2},{2,3},{3,4},{4,5},{5,6},{6,7},{7,8},{8,9},{9,10},{10,1... | collective-permute-start | bytes 3145736 | tf_op jit(solution)/shard_map/ppermute | solution.py:25
  198.7 33.2 %collective-permute-start.3 = (f32[4,4,128,128]{2,3,1,0:T(8,128)S(1)}, f32[4,4,128,128]{2,3,1,0:T(8,128)S(1)}, u32[]{:S(2)}, u32[]{:S(2)}) collective-permute-start(f32[4,4,128,128]{2,3,1,0:T(8,128)S(1)} %get-tuple-element.19), channel_id=1, source_target_pairs={{1,0},{2,1},{3,2},{4,3},{5,4},{6,5},{7,6},{8,7},{9,8},{10,9},{11,1... | collective-permute-start | bytes 3145736 | tf_op jit(solution)/shard_map/ppermute | solution.py:26
  209.0 22.9 %copy-start = (f32[5,128,128]{1,2,0:T(8,128)S(1)}, f32[5,128,128]{1,2,0:T(8,128)}, u32[]{:S(2)}) copy-start(f32[5,128,128]{1,2,0:T(8,128)} %get-tuple-element.8) | copy-start | bytes 983044
  209.0 22.9 %copy-start.1 = (f32[5,128,128]{1,2,0:T(8,128)S(1)}, f32[5,128,128]{1,2,0:T(8,128)}, u32[]{:S(2)}) copy-start(f32[5,128,128]{1,2,0:T(8,128)} %get-tuple-element.7) | copy-start | bytes 983044
  209.0 22.9 %copy-start.2 = (f32[5,128,128]{1,2,0:T(8,128)S(1)}, f32[5,128,128]{1,2,0:T(8,128)}, u32[]{:S(2)}) copy-start(f32[5,128,128]{1,2,0:T(8,128)} %get-tuple-element.5) | copy-start | bytes 983044
  209.0 22.9 %copy-start.3 = (f32[5,128,128]{1,2,0:T(8,128)S(1)}, f32[5,128,128]{1,2,0:T(8,128)}, u32[]{:S(2)}) copy-start(f32[5,128,128]{1,2,0:T(8,128)} %get-tuple-element.6) | copy-start | bytes 983044
  247.8 21.6 %collective-permute-start.4 = (f32[3,1,3,128,128]{3,4,2,1,0:T(8,128)S(1)}, f32[3,1,3,128,128]{3,4,2,1,0:T(8,128)S(1)}, u32[]{:S(2)}, u32[]{:S(2)}) collective-permute-start(f32[3,1,3,128,128]{3,4,2,1,0:T(8,128)S(1)} %get-tuple-element.20), channel_id=1, source_target_pairs={{0,1},{1,2},{2,3},{3,4},{4,5},{5,6},{6,7},{7,8},{8,9},{9,10},{10,1... | collective-permute-start | bytes 1769480 | tf_op jit(solution)/shard_map/ppermute | solution.py:25
  249.7 21.5 %collective-permute-start.5 = (f32[3,1,3,128,128]{3,4,2,1,0:T(8,128)S(1)}, f32[3,1,3,128,128]{3,4,2,1,0:T(8,128)S(1)}, u32[]{:S(2)}, u32[]{:S(2)}) collective-permute-start(f32[3,1,3,128,128]{3,4,2,1,0:T(8,128)S(1)} %get-tuple-element.21), channel_id=1, source_target_pairs={{1,0},{2,1},{3,2},{4,3},{5,4},{6,5},{7,6},{8,7},{9,8},{10,9},{11,1... | collective-permute-start | bytes 1769480 | tf_op jit(solution)/shard_map/ppermute | solution.py:26
  272.7 1.3 copy-start.4
Sparse Core Ops, SparseCore 0:
  39.3 155.7 all-reduce.4
where the time goes:
time: 282 us
  waiting for transfers between devices  198 us (70%)
  starting transfers between devices  37 us (13%)
  between operations  19 us (7%)
  matrix products  18.6 us (7%)
  other arithmetic  4.97 us (2%)
  local copies, waits for them, and re-layouts  3.94 us (1%)
    psum x1, waiting for transfers between devices, spread(): return lax.psum(jnp.where(mine, shard, jnp.zeros_like(shard)), axis)  156 us
    ppermute x3, waiting for transfers between devices, padded(): before = lax.ppermute(last, axis, up)  36.9 us
    ppermute x3, starting transfers between devices, padded(): after = lax.ppermute(first, axis, down)  31.2 us
    dot_general x15, matrix products, planes_xy(): jnp.einsum('wx,pxy->pwy', matrix_x, across, precision=lax.Precision.HIGHEST)  9.56 us
    dot_general x15, matrix products, planes_xy(): across = jnp.dot(field, matrix_y, precision=lax.Precision.HIGHEST)  9.09 us
    ppermute x3, starting transfers between devices, padded(): before = lax.ppermute(last, axis, up)  5.76 us
  transfers between devices with their start and end apart: 7, of which 7 were waited for; matrix products, arithmetic and copies ran while one was open for 1% of the time, Pallas kernels for 0%

commit v1 on v0

v1 whole, which is shorter than its diff:
```python
import math

import jax
import jax.numpy as jnp
from jax import lax
from jax.experimental import pallas as pl
from jax.experimental.pallas import tpu as pltpu
from jax.sharding import PartitionSpec as P

X = 128
Y = 128
ZD = 5
NSUB = 16
NREF = 4
WIN = 9
RG = 3
WDEN = 16
RAD = WIN // 2
ROWS = X // NSUB
EXT_R = ROWS + 2 * RAD
EXT_P = ZD + 2 * RAD
CELLS = ROWS * ZD
NF = 2 + NREF
MESH = pl.DeviceIdType.MESH

XA, XB, ZA, ZB, CA0, CA1, CB0, CB1, IA, IB, FA, FB = range(12)


def gauss_taps():
    raw = [math.exp(-0.5 * offset * offset) for offset in range(-RG, RG + 1)]
    total = sum(raw)
    return [value / total for value in raw]


def chunk_of(s, hi):
    y, x = s // 4, s % 4
    ys = y + hi * (3 - 2 * y)
    return 4 * ys + x + (ys % 2) * (3 - 2 * x)


def subject_of(c, hi):
    ys, xs = c // 4, c % 4
    x = xs + (ys % 2) * (3 - 2 * xs)
    return 4 * (ys + hi * (3 - 2 * ys)) + x


def window_depth(v):
    core = ((v[4] + v[5]) + (v[6] + v[7])) + v[8]
    suf2 = v[2] + v[3]
    suf1 = v[1] + suf2
    suf0 = v[0] + suf1
    pre2 = v[9] + v[10]
    pre3 = pre2 + v[11]
    pre4 = pre3 + v[12]
    return [core + suf0, (core + suf1) + v[9], (core + suf2) + pre2, (core + v[3]) + pre3, core + pre4]


def window_rows(v):
    suf = [None] * 8
    pre = [None] * 8
    suf[7] = v[7]
    pre[0] = v[8]
    for i in range(6, -1, -1):
        suf[i] = v[i] + suf[i + 1]
    for i in range(1, 8):
        pre[i] = pre[i - 1] + v[8 + i]
    return [suf[i] + pre[i] for i in range(8)]


def band(taps, dtype):
    radius = len(taps) // 2
    diff = lax.broadcasted_iota(jnp.int32, (128, 128), 0) - lax.broadcasted_iota(jnp.int32, (128, 128), 1)
    matrix = jnp.zeros((128, 128), jnp.float32)
    for offset in range(len(taps)):
        matrix = jnp.where(diff == offset - radius, taps[offset], matrix)
    return matrix.astype(dtype)


def coeff_kernel(
    idx_ref, w_ref, img, cf, ih,
    a_buf, w_buf, ext, zs, xs, bx, inv, dev, c_buf, cs,
    sa, ra, sw, rw, sr, rr, sh, rh,
):
    s = lax.axis_index("subj")
    d = lax.axis_index("depth")
    nd = lax.axis_size("depth")
    half = nd // 2
    hi = d // half
    c = chunk_of(s, hi)
    mirror = 4 * (3 - s // 4) + s % 4
    has_lo, has_up = d > 0, d < nd - 1
    cross_lo, cross_up = d == half, d == half - 1
    s_lo = jnp.where(cross_lo, mirror, s)
    s_up = jnp.where(cross_up, mirror, s)

    barrier = pltpu.get_barrier_semaphore()
    for k in range(1, NSUB):
        pl.semaphore_signal(barrier, inc=1, device_id=((s + k) % NSUB, d), device_id_type=MESH)

    @pl.when(has_lo)
    def _():
        pl.semaphore_signal(barrier, inc=1, device_id=(s_lo, d - 1), device_id_type=MESH)

    @pl.when(has_up)
    def _():
        pl.semaphore_signal(barrier, inc=1, device_id=(s_up, d + 1), device_id_type=MESH)

    @pl.when(cross_lo)
    def _():
        pl.semaphore_signal(barrier, inc=1, device_id=(s, d - 1), device_id_type=MESH)

    @pl.when(cross_up)
    def _():
        pl.semaphore_signal(barrier, inc=1, device_id=(s, d + 1), device_id_type=MESH)

    rows = lax.broadcasted_iota(jnp.int32, (8, 128), 0)
    wt = jnp.zeros((8, 128), jnp.float32)
    for r in range(NREF):
        wt = jnp.where(rows == r, w_ref[0, r].astype(jnp.float32) * (1.0 / WDEN), wt)
    w_buf[s] = wt

    @pl.when(c == 0)
    def _():
        ext[0:RAD] = jnp.zeros((RAD, EXT_P, NSUB, Y), jnp.float32)

    @pl.when(c == NSUB - 1)
    def _():
        ext[RAD + ROWS:] = jnp.zeros((RAD, EXT_P, NSUB, Y), jnp.float32)

    @pl.when(jnp.logical_not(has_lo))
    def _():
        ext[:, 0:RAD] = jnp.zeros((EXT_R, RAD, NSUB, Y), jnp.float32)
        ih[0:4] = jnp.zeros((4, X, Y), jnp.float32)
        cf[0:RG] = jnp.zeros((RG, NSUB, ROWS, Y), jnp.float32)

    @pl.when(jnp.logical_not(has_up))
    def _():
        ext[:, RAD + ZD:] = jnp.zeros((EXT_R, RAD, NSUB, Y), jnp.float32)
        ih[4:8] = jnp.zeros((4, X, Y), jnp.float32)
        cf[RG + ZD:] = jnp.zeros((RG, NSUB, ROWS, Y), jnp.float32)

    extra = has_lo.astype(jnp.int32) + has_up.astype(jnp.int32) + cross_lo.astype(jnp.int32) + cross_up.astype(jnp.int32)
    pl.semaphore_wait(barrier, NSUB - 1 + extra)

    def remote(src, dst, send, recv, device):
        return pltpu.make_async_remote_copy(
            src_ref=src, dst_ref=dst, send_sem=send, recv_sem=recv, device_id=device, device_id_type=MESH
        )

    def chunk_out(k):
        to = (s + k) % NSUB
        return remote(img.at[:, chunk_of(to, hi)], a_buf.at[s], sa.at[k], ra.at[s], (to, d))

    def chunk_in(k):
        frm = (s + NSUB - k) % NSUB
        return remote(img.at[:, 0], a_buf.at[frm], sa.at[k], ra.at[frm], (frm, d))

    def weight_out(k):
        to = (s + k) % NSUB
        return remote(w_buf.at[s], w_buf.at[s], sw.at[k], rw.at[s], (to, d))

    def weight_in(k):
        frm = (s + NSUB - k) % NSUB
        return remote(w_buf.at[frm], w_buf.at[frm], sw.at[k], rw.at[frm], (frm, d))

    for k in range(1, NSUB):
        chunk_out(k).start()
    for k in range(1, NSUB):
        weight_out(k).start()
    a_buf[s] = img[:, c]
    for k in range(1, NSUB):
        chunk_in(k).wait_recv()

    a_flat = a_buf.reshape(NSUB * ZD * ROWS, Y)
    for p in range(ZD):
        for r in range(ROWS):
            ext[RAD + r, RAD + p] = a_flat[pl.ds(p * ROWS + r, NSUB, stride=ZD * ROWS), :]

    prev, nxt = subject_of(jnp.maximum(c - 1, 0), hi), subject_of(jnp.minimum(c + 1, NSUB - 1), hi)
    core_p = pl.ds(RAD, ZD)
    core_r = pl.ds(RAD, ROWS)
    last = RAD + ROWS
    x_dn = remote(ext.at[pl.ds(RAD, RAD), core_p], ext.at[pl.ds(last, RAD), core_p], sh.at[XA], rh.at[XA], (prev, d))
    x_up = remote(ext.at[pl.ds(ROWS, RAD), core_p], ext.at[pl.ds(0, RAD), core_p], sh.at[XB], rh.at[XB], (nxt, d))

    def z_dn(block, sem):
        return remote(ext.at[block, pl.ds(RAD, RAD)], ext.at[block, pl.ds(RAD + ZD, RAD)], sh.at[sem], rh.at[sem], (s_lo, d - 1))

    def z_up(block, sem):
        return remote(ext.at[block, pl.ds(ZD, RAD)], ext.at[block, pl.ds(0, RAD)], sh.at[sem], rh.at[sem], (s_up, d + 1))

    i_dn = remote(img.reshape(ZD, X, Y).at[pl.ds(0, 4)], ih.at[pl.ds(4, 4)], sh.at[IA], rh.at[IA], (s, d - 1))
    i_up = remote(img.reshape(ZD, X, Y).at[pl.ds(1, 4)], ih.at[pl.ds(0, 4)], sh.at[IB], rh.at[IB], (s, d + 1))
    has_prev, has_next = c > 0, c < NSUB - 1
    top, bottom = pl.ds(0, RAD), pl.ds(last, RAD)

    @pl.when(has_lo)
    def _():
        z_dn(core_r, ZA).start()

    @pl.when(has_up)
    def _():
        z_up(core_r, ZB).start()

    @pl.when(has_prev)
    def _():
        x_dn.start()

    @pl.when(has_next)
    def _():
        x_up.start()

    @pl.when(has_next)
    def _():
        x_dn.wait_recv()

        @pl.when(has_lo)
        def _():
            z_dn(bottom, CA1).start()

        @pl.when(has_up)
        def _():
            z_up(bottom, CB1).start()

    @pl.when(has_prev)
    def _():
        x_up.wait_recv()

        @pl.when(has_lo)
        def _():
            z_dn(top, CA0).start()

        @pl.when(has_up)
        def _():
            z_up(top, CB0).start()

    @pl.when(has_lo)
    def _():
        i_dn.start()

    @pl.when(has_up)
    def _():
        i_up.start()

    @pl.when(has_up)
    def _():
        z_dn(core_r, ZA).wait_recv()

        @pl.when(has_prev)
        def _():
            z_dn(top, CA0).wait_recv()

        @pl.when(has_next)
        def _():
            z_dn(bottom, CA1).wait_recv()

    @pl.when(has_lo)
    def _():
        z_up(core_r, ZB).wait_recv()

        @pl.when(has_prev)
        def _():
            z_up(top, CB0).wait_recv()

        @pl.when(has_next)
        def _():
            z_up(bottom, CB1).wait_recv()

    refs = [idx_ref[r] for r in range(NREF)]

    def depth_pass(row, carry):
        vals = [ext[row, p] for p in range(EXT_P)]
        for k, total in enumerate(window_depth(vals)):
            zs[0, row, k] = total
        for k, total in enumerate(window_depth([v * v for v in vals])):
            zs[1, row, k] = total
        for r in range(NREF):
            prods = [vals[p] * ext[row, p, pl.ds(refs[r], 1), :] for p in range(EXT_P)]
            for k, total in enumerate(window_depth(prods)):
                zs[2 + r, row, k] = total
        return carry

    lax.fori_loop(0, EXT_R, depth_pass, 0)

    def row_pass(f, carry):
        for k in range(ZD):
            for r, total in enumerate(window_rows([zs[f, row, k] for row in range(EXT_R)])):
                xs[f * CELLS + r * ZD + k] = total
        return carry

    lax.fori_loop(0, NF, row_pass, 0)

    ones = band([1.0] * WIN, jnp.bfloat16)
    ones2 = jnp.concatenate([ones, ones], axis=0)

    def lane_pass(b, carry):
        val = xs[pl.ds(b * 20, 20)].reshape(320, Y)
        high = val.astype(jnp.bfloat16)
        rest = val - high.astype(jnp.float32)
        mid = rest.astype(jnp.bfloat16)
        low = (rest - mid.astype(jnp.float32)).astype(jnp.bfloat16)
        total = jnp.dot(jnp.concatenate([high, mid], axis=1), ones2, preferred_element_type=jnp.float32)
        total = total + jnp.dot(low, ones, preferred_element_type=jnp.float32)
        bx[pl.ds(b * 20, 20)] = (total * (1.0 / WIN**3)).reshape(20, NSUB, Y)
        return carry

    lax.fori_loop(0, NF * CELLS // 20, lane_pass, 0)

    def stats(r, carry):
        for k in range(ZD):
            q = r * ZD + k
            mean = bx[q]
            inv[q] = 1.0 / (bx[CELLS + q] - mean * mean + 1e-5)
            dev[q] = ext[RAD + r, RAD + k] - mean
        return carry

    lax.fori_loop(0, ROWS, stats, 0)

    for k in range(1, NSUB):
        weight_in(k).wait_recv()
    w_flat = w_buf.reshape(NSUB * 8, 128)
    weights = [w_flat[pl.ds(r, NSUB, stride=8), :] for r in range(NREF)]

    def combine(row, carry):
        for k in range(ZD):
            q = row * ZD + k
            mean_i, inv_i, dev_i = bx[q], inv[q], dev[q]
            total = None
            for r in range(NREF):
                one = pl.ds(refs[r], 1)
                gain = (bx[(2 + r) * CELLS + q] - mean_i * bx[q, one, :]) * inv_i
                term = (2.0 * gain * inv[q, one, :]) * (dev[q, one, :] - gain * dev_i) * weights[r]
                total = term if total is None else total + term
            c_buf[pl.ds(q * NSUB, NSUB), :] = total
        return carry

    lax.fori_loop(0, ROWS, combine, 0)

    for sub in range(NSUB):
        for p in range(ZD):
            cs[sub, p] = c_buf[pl.ds(p * NSUB + sub, ROWS, stride=ZD * NSUB), :]

    planes = pl.ds(RG, ZD)

    def back_out(k):
        to = (s + k) % NSUB
        return remote(cs.at[to], cf.at[planes, c], sr.at[k], rr.at[c], (to, d))

    def back_in(k):
        frm = (s + NSUB - k) % NSUB
        chunk = chunk_of(frm, hi)
        return remote(cs.at[frm], cf.at[planes, chunk], sr.at[k], rr.at[chunk], (frm, d))

    for k in range(1, NSUB):
        back_out(k).start()
    cf[planes, c] = cs[s]
    for k in range(1, NSUB):
        back_in(k).wait_recv()

    f_dn = remote(cf.at[pl.ds(RG, RG)], cf.at[pl.ds(RG + ZD, RG)], sh.at[FA], rh.at[FA], (s, d - 1))
    f_up = remote(cf.at[pl.ds(ZD, RG)], cf.at[pl.ds(0, RG)], sh.at[FB], rh.at[FB], (s, d + 1))

    @pl.when(has_lo)
    def _():
        f_dn.start()

    @pl.when(has_up)
    def _():
        f_up.start()

    for k in range(1, NSUB):
        chunk_out(k).wait_send()
        weight_out(k).wait_send()
        back_out(k).wait_send()

    @pl.when(has_prev)
    def _():
        x_dn.wait_send()

    @pl.when(has_next)
    def _():
        x_up.wait_send()

    @pl.when(has_lo)
    def _():
        z_dn(core_r, ZA).wait_send()
        i_dn.wait_send()
        i_up.wait_recv()

        @pl.when(has_prev)
        def _():
            z_dn(top, CA0).wait_send()

        @pl.when(has_next)
        def _():
            z_dn(bottom, CA1).wait_send()

    @pl.when(has_up)
    def _():
        z_up(core_r, ZB).wait_send()
        i_up.wait_send()
        i_dn.wait_recv()

        @pl.when(has_prev)
        def _():
            z_up(top, CB0).wait_send()

        @pl.when(has_next)
        def _():
            z_up(bottom, CB1).wait_send()

    @pl.when(has_lo)
    def _():
        f_dn.wait_send()
        f_up.wait_recv()

    @pl.when(has_up)
    def _():
        f_up.wait_send()
        f_dn.wait_recv()


def smooth_kernel(cf, img, ih, vel, out, force):
    taps = gauss_taps()
    lane = lax.broadcasted_iota(jnp.int32, (X, Y), 1)
    row = lax.broadcasted_iota(jnp.int32, (X, Y), 0)

    def plane(i):
        if i < 4:
            return ih[i]
        if i < 4 + ZD:
            return img[i - 4]
        return ih[i - ZD]

    for p in range(ZD + 2 * RG):
        coef = cf[p] * 0.5
        here = plane(p + 1)
        force[0, p] = coef * (plane(p + 2) - plane(p))
        below = jnp.where(row == X - 1, 0.0, pltpu.roll(here, X - 1, 0))
        above = jnp.where(row == 0, 0.0, pltpu.roll(here, 1, 0))
        force[1, p] = coef * (below - above)
        after = jnp.where(lane == Y - 1, 0.0, pltpu.roll(here, Y - 1, 1))
        before = jnp.where(lane == 0, 0.0, pltpu.roll(here, 1, 1))
        force[2, p] = coef * (after - before)

    matrix = band(taps, jnp.float32)
    t_high = matrix.astype(jnp.bfloat16)
    t_low = (matrix - t_high.astype(jnp.float32)).astype(jnp.bfloat16)
    none = jnp.zeros((128, 128), jnp.bfloat16)
    right = jnp.concatenate(
        [jnp.concatenate([t_high, t_low], axis=1), jnp.concatenate([t_high, none], axis=1)], axis=0
    )
    left = jnp.concatenate(
        [jnp.concatenate([t_high, t_high], axis=1), jnp.concatenate([t_low, none], axis=1)], axis=0
    )

    def split(val):
        high = val.astype(jnp.bfloat16)
        return high, (val - high.astype(jnp.float32)).astype(jnp.bfloat16)

    def body(comp, carry):
        for p in range(ZD):
            total = taps[RG] * force[comp, p + RG]
            for k in range(1, RG + 1):
                total = total + taps[RG + k] * (force[comp, p + RG - k] + force[comp, p + RG + k])
            both = jnp.dot(jnp.concatenate(split(total), axis=1), right, preferred_element_type=jnp.float32)
            across = both[:, :Y] + both[:, Y:]
            both = jnp.dot(left, jnp.concatenate(split(across), axis=0), preferred_element_type=jnp.float32)
            out[comp, p] = vel[comp, p] + 40.0 * (both[:X] + both[X:])
        return carry

    lax.fori_loop(0, 3, body, 0)


def on_device(images, velocity, ref_index, ref_weights):
    vmem = pl.BlockSpec(memory_space=pltpu.VMEM)
    smem = pl.BlockSpec(memory_space=pltpu.SMEM)
    f32 = jnp.float32
    dma = pltpu.SemaphoreType.DMA
    cf, ih = pl.pallas_call(
        coeff_kernel,
        out_shape=(
            jax.ShapeDtypeStruct((ZD + 2 * RG, NSUB, ROWS, Y), f32),
            jax.ShapeDtypeStruct((8, X, Y), f32),
        ),
        in_specs=[smem, smem, vmem],
        out_specs=(vmem, vmem),
        scratch_shapes=[
            pltpu.VMEM((NSUB, ZD, ROWS, Y), f32),
            pltpu.VMEM((NSUB, 8, 128), f32),
            pltpu.VMEM((EXT_R, EXT_P, NSUB, Y), f32),
            pltpu.VMEM((NF, EXT_R, ZD, NSUB, Y), f32),
            pltpu.VMEM((NF * CELLS, NSUB, Y), f32),
            pltpu.VMEM((NF * CELLS, NSUB, Y), f32),
            pltpu.VMEM((CELLS, NSUB, Y), f32),
            pltpu.VMEM((CELLS, NSUB, Y), f32),
            pltpu.VMEM((CELLS * NSUB, Y), f32),
            pltpu.VMEM((NSUB, ZD, ROWS, Y), f32),
            dma((NSUB,)), dma((NSUB,)), dma((NSUB,)), dma((NSUB,)), dma((NSUB,)), dma((NSUB,)),
            dma((12,)), dma((12,)),
        ],
        compiler_params=pltpu.CompilerParams(
            collective_id=0, has_side_effects=True, vmem_limit_bytes=32 * 1024 * 1024
        ),
    )(ref_index, ref_weights, images.reshape(ZD, NSUB, ROWS, Y))
    out = pl.pallas_call(
        smooth_kernel,
        out_shape=jax.ShapeDtypeStruct((3, ZD, X, Y), f32),
        in_specs=[vmem] * 4,
        out_specs=vmem,
        scratch_shapes=[pltpu.VMEM((3, ZD + 2 * RG, X, Y), f32)],
        compiler_params=pltpu.CompilerParams(vmem_limit_bytes=32 * 1024 * 1024),
    )(cf.reshape(ZD + 2 * RG, X, Y), images.reshape(ZD, X, Y), ih, velocity.reshape(3, ZD, X, Y))
    return out.reshape(3, 1, ZD, X, Y)


def solution(mesh):
    placed = (
        P("subj", "depth", None, None),
        P(None, "subj", "depth", None, None),
        P(),
        P("subj", None),
    )
    return jax.shard_map(
        on_device,
        mesh=mesh,
        in_specs=placed,
        out_specs=P(None, "subj", "depth", None, None),
        check_vma=False,
    )
```

time: 282 us -> 66.1 us (0.23)
  the two profiles are of different devices: /device:TPU:48 before, /device:TPU:56 now
where the time goes in v1:
time: 66.1 us; the launch traced here: 65.9 us
  Pallas kernels  63 us (95%)
  local copies, waits for them, and re-layouts  2.84 us (4%)
    pallas_call x1, Pallas kernels, on_device(): pl.pallas_call(coeff_kernel, out_shape=(jax.ShapeDtypeStruct((ZD + 2 * RG...  59.4 us
    pallas_call x1, Pallas kernels, on_device(): pl.pallas_call(smooth_kernel, out_shape=jax.ShapeDtypeStruct((3, ZD, X, Y...  3.59 us
    unnamed x10, local copies, waits for them, and re-layouts  2.84 us

profile of v1, /device:TPU:56, one launch (start us, length us, event | category | flops | bytes accessed | tf_op | source)
XLA Modules:
  0.0 65.9 jit_solution(14310964558633185700)
XLA Ops:
  0.0 0.0 copy-start.3
  0.0 0.0 copy-start.4
  0.0 0.7 copy-done.3
  0.7 0.0 copy-done.4
  0.7 0.0 copy-start
  0.7 1.0 %copy-done = f32[1,5,128,128]{3,2,1,0:T(8,128)S(1)} copy-done((f32[1,5,128,128]{3,2,1,0:T(8,128)S(1)}, f32[1,5,128,128]{3,2,1,0:T(8,128)}, u32[]{:S(2)}) %copy-start) | copy-done | bytes 327704
  1.6 0.0 copy-start.1
  1.6 59.4 %shard_map.46 = (f32[11,16,8,128]{3,2,1,0:T(8,128)S(1)}, f32[8,128,128]{2,1,0:T(8,128)S(1)}) custom-call(s32[4]{0:T(128)S(1)} %copy-done.3, s32[1,4]{1,0:T(1,128)S(1)} %copy-done.4, f32[5,16,8,128]{3,2,1,0:T(8,128)S(1)} %bitcast.7), custom_call_target="tpu_custom_call" | custom-call | tf_op jit(solution)/shard_map/pallas_call | solution.py:480
  61.1 0.0 copy-done.1
  61.1 0.0 copy-start.2
  61.1 1.2 %copy-done.2 = f32[3,1,5,128,128]{4,3,2,1,0:T(8,128)S(1)} copy-done((f32[3,1,5,128,128]{4,3,2,1,0:T(8,128)S(1)}, f32[3,1,5,128,128]{4,3,2,1,0:T(8,128)}, u32[]{:S(2)}) %copy-start.2) | copy-done | bytes 983064
  62.3 3.6 %shard_map.47 = f32[3,5,128,128]{3,2,1,0:T(8,128)} custom-call(f32[11,128,128]{2,1,0:T(8,128)S(1)} %bitcast.10, f32[5,128,128]{2,1,0:T(8,128)S(1)} %bitcast.8, f32[8,128,128]{2,1,0:T(8,128)S(1)} %get-tuple-element.8.ih, f32[3,5,128,128]{3,2,1,0:T(8,128)S(1)} %bitcast.9), custom_call_target="tpu_custom_call" | custom-call | tf_op jit(solution)/shard_map/pallas_call | solution.py:506
Async XLA Ops:
  0.0 0.7 copy-start.3
  0.0 0.7 %copy-start.4 = (s32[1,4]{1,0:T(1,128)S(1)}, s32[1,4]{1,0:T(1,128)}, u32[]{:S(2)}) copy-start(s32[1,4]{1,0:T(1,128)} %w_ref.1) | copy-start | bytes 52
  0.7 1.0 %copy-start = (f32[1,5,128,128]{3,2,1,0:T(8,128)S(1)}, f32[1,5,128,128]{3,2,1,0:T(8,128)}, u32[]{:S(2)}) copy-start(f32[1,5,128,128]{3,2,1,0:T(8,128)} %param.4) | copy-start | bytes 983044
  1.6 59.4 %copy-start.1 = (f32[1,5,128,128]{3,2,1,0:T(8,128)S(1)}, f32[1,5,128,128]{3,2,1,0:T(8,128)}, u32[]{:S(2)}) copy-start(f32[1,5,128,128]{3,2,1,0:T(8,128)} %param.4) | copy-start | bytes 983044
  61.1 1.2 %copy-start.2 = (f32[3,1,5,128,128]{4,3,2,1,0:T(8,128)S(1)}, f32[3,1,5,128,128]{4,3,2,1,0:T(8,128)}, u32[]{:S(2)}) copy-start(f32[3,1,5,128,128]{4,3,2,1,0:T(8,128)} %param.5) | copy-start | bytes 2949124

commit v2 on v1

v2 whole, which is shorter than its diff:
```python
import functools
import math

import jax
import jax.numpy as jnp
from jax import lax
from jax.experimental import pallas as pl
from jax.experimental.pallas import tpu as pltpu
from jax.sharding import PartitionSpec as P

X = 128
Y = 128
ZD = 5
NSUB = 16
NREF = 4
WIN = 9
RG = 3
WDEN = 16
RAD = WIN // 2
ROWS = X // NSUB
EXT_R = ROWS + 2 * RAD
EXT_P = ZD + 2 * RAD
CELLS = ROWS * ZD
NF = 2 + NREF
MESH = pl.DeviceIdType.MESH

XA, XB, ZA, ZB, CA0, CA1, CB0, CB1, IA, IB, FA, FB, YA, YB = range(14)


def gauss_taps():
    raw = [math.exp(-0.5 * offset * offset) for offset in range(-RG, RG + 1)]
    total = sum(raw)
    return [value / total for value in raw]


def chunk_of(s, hi):
    y, x = s // 4, s % 4
    ys = y + hi * (3 - 2 * y)
    return 4 * ys + x + (ys % 2) * (3 - 2 * x)


def subject_of(c, hi):
    ys, xs = c // 4, c % 4
    x = xs + (ys % 2) * (3 - 2 * xs)
    return 4 * (ys + hi * (3 - 2 * ys)) + x


def window_depth(v):
    core = ((v[4] + v[5]) + (v[6] + v[7])) + v[8]
    suf2 = v[2] + v[3]
    suf1 = v[1] + suf2
    suf0 = v[0] + suf1
    pre2 = v[9] + v[10]
    pre3 = pre2 + v[11]
    pre4 = pre3 + v[12]
    return [core + suf0, (core + suf1) + v[9], (core + suf2) + pre2, (core + v[3]) + pre3, core + pre4]


def window_rows(v):
    suf = [None] * 8
    pre = [None] * 8
    suf[7] = v[7]
    pre[0] = v[8]
    for i in range(6, -1, -1):
        suf[i] = v[i] + suf[i + 1]
    for i in range(1, 8):
        pre[i] = pre[i - 1] + v[8 + i]
    return [suf[i] + pre[i] for i in range(8)]


def band(taps, dtype):
    radius = len(taps) // 2
    diff = lax.broadcasted_iota(jnp.int32, (128, 128), 0) - lax.broadcasted_iota(jnp.int32, (128, 128), 1)
    matrix = jnp.zeros((128, 128), jnp.float32)
    for offset in range(len(taps)):
        matrix = jnp.where(diff == offset - radius, taps[offset], matrix)
    return matrix.astype(dtype)


def coeff_kernel(
    idx_ref, w_ref, img_hbm, cf, ih,
    img, a_buf, w_buf, ext, ext_top, ext_bot, zs, xs, bx, inv, dev, c_buf, cs, hs,
    sa, ra, sw, rw, sr, rr, sg, rg, sc, rc, sh, rh, load_sem,
):
    s = lax.axis_index("subj")
    d = lax.axis_index("depth")
    nd = lax.axis_size("depth")
    half = nd // 2
    hi = d // half
    c = chunk_of(s, hi)
    mirror = 4 * (3 - s // 4) + s % 4
    has_lo, has_up = d > 0, d < nd - 1
    cross_lo, cross_up = d == half, d == half - 1
    near_lo, near_up = has_lo & (d != half), has_up & (d != half - 1)
    has_prev, has_next = c > 0, c < NSUB - 1
    s_lo = jnp.where(cross_lo, mirror, s)
    s_up = jnp.where(cross_up, mirror, s)

    load = pltpu.make_async_copy(img_hbm, img, load_sem)
    load.start()

    barrier = pltpu.get_barrier_semaphore()
    for k in range(1, NSUB):
        pl.semaphore_signal(barrier, inc=1, device_id=((s + k) % NSUB, d), device_id_type=MESH)

    @pl.when(near_lo)
    def _():
        pl.semaphore_signal(barrier, inc=1, device_id=(s, d - 1), device_id_type=MESH)

    @pl.when(near_up)
    def _():
        pl.semaphore_signal(barrier, inc=1, device_id=(s, d + 1), device_id_type=MESH)

    @pl.when(cross_lo)
    def _():
        for k in range(NSUB):
            pl.semaphore_signal(barrier, inc=1, device_id=((s + k) % NSUB, d - 1), device_id_type=MESH)

    @pl.when(cross_up)
    def _():
        for k in range(NSUB):
            pl.semaphore_signal(barrier, inc=1, device_id=((s + k) % NSUB, d + 1), device_id_type=MESH)

    rows = lax.broadcasted_iota(jnp.int32, (8, 128), 0)
    wt = jnp.zeros((8, 128), jnp.float32)
    for r in range(NREF):
        wt = jnp.where(rows == r, w_ref[0, r].astype(jnp.float32) * (1.0 / WDEN), wt)
    w_buf[s] = wt

    @pl.when(c == 0)
    def _():
        ext_top[...] = jnp.zeros((RAD, EXT_P, NSUB, Y), jnp.float32)

    @pl.when(c == NSUB - 1)
    def _():
        ext_bot[...] = jnp.zeros((RAD, EXT_P, NSUB, Y), jnp.float32)

    @pl.when(jnp.logical_not(has_lo))
    def _():
        ext[:, 0:RAD] = jnp.zeros((ROWS, RAD, NSUB, Y), jnp.float32)
        ext_top[:, 0:RAD] = jnp.zeros((RAD, RAD, NSUB, Y), jnp.float32)
        ext_bot[:, 0:RAD] = jnp.zeros((RAD, RAD, NSUB, Y), jnp.float32)
        ih[0:4] = jnp.zeros((4, NSUB, ROWS, Y), jnp.float32)
        cf[0:RG] = jnp.zeros((RG, NSUB, ROWS, Y), jnp.float32)

    @pl.when(jnp.logical_not(has_up))
    def _():
        ext[:, RAD + ZD:] = jnp.zeros((ROWS, RAD, NSUB, Y), jnp.float32)
        ext_top[:, RAD + ZD:] = jnp.zeros((RAD, RAD, NSUB, Y), jnp.float32)
        ext_bot[:, RAD + ZD:] = jnp.zeros((RAD, RAD, NSUB, Y), jnp.float32)
        ih[4:8] = jnp.zeros((4, NSUB, ROWS, Y), jnp.float32)
        cf[RG + ZD:] = jnp.zeros((RG, NSUB, ROWS, Y), jnp.float32)

    load.wait()
    one_if = lambda cond: cond.astype(jnp.int32)
    extra = one_if(near_lo) + one_if(near_up) + NSUB * (one_if(cross_lo) + one_if(cross_up))
    pl.semaphore_wait(barrier, NSUB - 1 + extra)

    def remote(src, dst, send, recv, device):
        return pltpu.make_async_remote_copy(
            src_ref=src, dst_ref=dst, send_sem=send, recv_sem=recv, device_id=device, device_id_type=MESH
        )

    def peer_to(k):
        return (s + k) % NSUB

    def peer_from(k):
        return (s + NSUB - k) % NSUB

    def chunk_out(k):
        to = peer_to(k)
        return remote(img.at[:, chunk_of(to, hi)], a_buf.at[s], sa.at[k], ra.at[s], (to, d))

    def chunk_in(k):
        frm = peer_from(k)
        return remote(img.at[:, 0], a_buf.at[frm], sa.at[k], ra.at[frm], (frm, d))

    def weight_out(k):
        return remote(w_buf.at[s], w_buf.at[s], sw.at[k], rw.at[s], (peer_to(k), d))

    def weight_in(k):
        frm = peer_from(k)
        return remote(w_buf.at[frm], w_buf.at[frm], sw.at[k], rw.at[frm], (frm, d))

    def spread():
        for k in range(1, NSUB):
            chunk_out(k).start()
        for k in range(1, NSUB):
            weight_out(k).start()
        a_buf[s] = img[:, c]
        for k in range(1, NSUB):
            chunk_in(k).wait_recv()
        a_flat = a_buf.reshape(NSUB * ZD * ROWS, Y)
        for p in range(ZD):
            for r in range(ROWS):
                ext[r, RAD + p] = a_flat[pl.ds(p * ROWS + r, NSUB, stride=ZD * ROWS), :]

    prev, nxt = subject_of(jnp.maximum(c - 1, 0), hi), subject_of(jnp.minimum(c + 1, NSUB - 1), hi)
    core_p = pl.ds(RAD, ZD)
    low_p, high_p = pl.ds(0, RAD), pl.ds(RAD + ZD, RAD)

    def x_dn(planes, send, recv):
        return remote(ext.at[pl.ds(0, RAD), planes], ext_bot.at[:, planes], sh.at[send], rh.at[recv], (prev, d))

    def x_up(planes, send, recv):
        return remote(ext.at[pl.ds(RAD, RAD), planes], ext_top.at[:, planes], sh.at[send], rh.at[recv], (nxt, d))

    def z_dn(block, sem):
        return remote(block.at[:, pl.ds(RAD, RAD)], block.at[:, high_p], sh.at[sem], rh.at[sem], (s_lo, d - 1))

    def z_up(block, sem):
        return remote(block.at[:, pl.ds(ZD, RAD)], block.at[:, low_p], sh.at[sem], rh.at[sem], (s_up, d + 1))

    def i_dn():
        return remote(img.at[pl.ds(0, 4)], ih.at[pl.ds(4, 4)], sh.at[IA], rh.at[IA], (s, d - 1))

    def i_up():
        return remote(img.at[pl.ds(1, 4)], ih.at[pl.ds(0, 4)], sh.at[IB], rh.at[IB], (s, d + 1))

    def across_dn_x(go):
        @pl.when(has_prev)
        def _():
            @pl.when(cross_up)
            def _():
                go(x_dn(high_p, YA, CA1))

            @pl.when(cross_lo)
            def _():
                go(x_dn(low_p, YA, CB1))

    def across_up_x(go):
        @pl.when(has_next)
        def _():
            @pl.when(cross_up)
            def _():
                go(x_up(high_p, YB, CA0))

            @pl.when(cross_lo)
            def _():
                go(x_up(low_p, YB, CB0))

    def halo_start():
        @pl.when(has_lo)
        def _():
            z_dn(ext, ZA).start()

        @pl.when(has_up)
        def _():
            z_up(ext, ZB).start()

        @pl.when(has_prev)
        def _():
            x_dn(core_p, XA, XA).start()

        @pl.when(has_next)
        def _():
            x_up(core_p, XB, XB).start()

        @pl.when(has_next)
        def _():
            x_dn(core_p, XA, XA).wait_recv()

            @pl.when(near_lo)
            def _():
                z_dn(ext_bot, CA1).start()

            @pl.when(near_up)
            def _():
                z_up(ext_bot, CB1).start()

        @pl.when(has_prev)
        def _():
            x_up(core_p, XB, XB).wait_recv()

            @pl.when(near_lo)
            def _():
                z_dn(ext_top, CA0).start()

            @pl.when(near_up)
            def _():
                z_up(ext_top, CB0).start()

        @pl.when(has_up)
        def _():
            z_dn(ext, ZA).wait_recv()

        @pl.when(has_lo)
        def _():
            z_up(ext, ZB).wait_recv()

        across_dn_x(lambda copy: copy.start())
        across_up_x(lambda copy: copy.start())

        @pl.when(near_lo)
        def _():
            i_dn().start()

        @pl.when(near_up)
        def _():
            i_up().start()

    e_flat = ext.reshape(ROWS * EXT_P * NSUB, Y)

    def slab_out(k, first):
        to = peer_to(k)
        return remote(hs.at[to], ih.at[pl.ds(first, 4), c], sg.at[k], rg.at[c], (to, d))

    def slab_in(k, first):
        frm = peer_from(k)
        chunk = chunk_of(frm, hi)
        return remote(hs.at[frm], ih.at[pl.ds(first, 4), chunk], sg.at[k], rg.at[chunk], (frm, d))

    def slab_start(base, first):
        for sub in range(NSUB):
            for p in range(4):
                at = (base + p) * NSUB + sub
                hs[sub, p] = e_flat[pl.ds(at, ROWS, stride=EXT_P * NSUB), :]
        for k in range(1, NSUB):
            slab_out(k, first).start()
        ih[pl.ds(first, 4), c] = hs[s]

    def slabs():
        @pl.when(cross_lo)
        def _():
            slab_start(0, 0)

        @pl.when(cross_up)
        def _():
            slab_start(RAD + ZD, 4)

    def corners_end():
        @pl.when(has_up)
        def _():
            @pl.when(has_prev)
            def _():
                z_dn(ext_top, CA0).wait_recv()

            @pl.when(has_next)
            def _():
                z_dn(ext_bot, CA1).wait_recv()

        @pl.when(has_lo)
        def _():
            @pl.when(has_prev)
            def _():
                z_up(ext_top, CB0).wait_recv()

            @pl.when(has_next)
            def _():
                z_up(ext_bot, CB1).wait_recv()

    refs = [idx_ref[r] for r in range(NREF)]

    def depth_pass(block, first, row, carry):
        at = row + first
        vals = [block[row, p] for p in range(EXT_P)]
        for k, total in enumerate(window_depth(vals)):
            zs[0, at, k] = total
        for k, total in enumerate(window_depth([v * v for v in vals])):
            zs[1, at, k] = total
        for r in range(NREF):
            prods = [vals[p] * block[row, p, pl.ds(refs[r], 1), :] for p in range(EXT_P)]
            for k, total in enumerate(window_depth(prods)):
                zs[2 + r, at, k] = total
        return carry

    def row_pass(f, carry):
        for k in range(ZD):
            for r, total in enumerate(window_rows([zs[f, row, k] for row in range(EXT_R)])):
                xs[f * CELLS + r * ZD + k] = total
        return carry

    def core_rows():
        lax.fori_loop(0, ROWS, functools.partial(depth_pass, ext, RAD), 0)

    def other_rows():
        lax.fori_loop(0, RAD, functools.partial(depth_pass, ext_top, 0), 0)
        lax.fori_loop(0, RAD, functools.partial(depth_pass, ext_bot, RAD + ROWS), 0)

    def boxes():
        lax.fori_loop(0, NF, row_pass, 0)
        ones = band([1.0] * WIN, jnp.bfloat16)
        ones2 = jnp.concatenate([ones, ones], axis=0)

        def lane_pass(b, carry):
            val = xs[pl.ds(b * 20, 20)].reshape(320, Y)
            high = val.astype(jnp.bfloat16)
            rest = val - high.astype(jnp.float32)
            mid = rest.astype(jnp.bfloat16)
            low = (rest - mid.astype(jnp.float32)).astype(jnp.bfloat16)
            total = jnp.dot(jnp.concatenate([high, mid], axis=1), ones2, preferred_element_type=jnp.float32)
            total = total + jnp.dot(low, ones, preferred_element_type=jnp.float32)
            bx[pl.ds(b * 20, 20)] = (total * (1.0 / WIN**3)).reshape(20, NSUB, Y)
            return carry

        lax.fori_loop(0, NF * CELLS // 20, lane_pass, 0)

    def combined():
        def stats(r, carry):
            for k in range(ZD):
                q = r * ZD + k
                mean = bx[q]
                inv[q] = 1.0 / (bx[CELLS + q] - mean * mean + 1e-5)
                dev[q] = ext[r, RAD + k] - mean
            return carry

        lax.fori_loop(0, ROWS, stats, 0)
        for k in range(1, NSUB):
            weight_in(k).wait_recv()
        w_flat = w_buf.reshape(NSUB * 8, 128)
        weights = [w_flat[pl.ds(r, NSUB, stride=8), :] for r in range(NREF)]

        def combine(row, carry):
            for k in range(ZD):
                q = row * ZD + k
                mean_i, inv_i, dev_i = bx[q], inv[q], dev[q]
                total = None
                for r in range(NREF):
                    one = pl.ds(refs[r], 1)
                    gain = (bx[(2 + r) * CELLS + q] - mean_i * bx[q, one, :]) * inv_i
                    term = (2.0 * gain * inv[q, one, :]) * (dev[q, one, :] - gain * dev_i) * weights[r]
                    total = term if total is None else total + term
                c_buf[pl.ds(q * NSUB, NSUB), :] = total
            return carry

        lax.fori_loop(0, ROWS, combine, 0)
        for sub in range(NSUB):
            for p in range(ZD):
                cs[sub, p] = c_buf[pl.ds(p * NSUB + sub, ROWS, stride=ZD * NSUB), :]

    planes = pl.ds(RG, ZD)

    def back_out(k):
        to = peer_to(k)
        return remote(cs.at[to], cf.at[planes, c], sr.at[k], rr.at[c], (to, d))

    def back_in(k):
        frm = peer_from(k)
        chunk = chunk_of(frm, hi)
        return remote(cs.at[frm], cf.at[planes, chunk], sr.at[k], rr.at[chunk], (frm, d))

    def over_up(k):
        to = peer_to(k)
        return remote(cs.at[to, pl.ds(2, RG)], cf.at[pl.ds(0, RG), c], sc.at[k], rc.at[c], (to, d + 1))

    def over_dn(k):
        to = peer_to(k)
        return remote(cs.at[to, pl.ds(0, RG)], cf.at[pl.ds(RG + ZD, RG), c], sc.at[k], rc.at[c], (to, d - 1))

    def over_in(k, first, side):
        return remote(cs.at[k, pl.ds(0, RG)], cf.at[pl.ds(first, RG), k], sc.at[k], rc.at[k], (s, side))

    def f_dn():
        return remote(cf.at[pl.ds(RG, RG)], cf.at[pl.ds(RG + ZD, RG)], sh.at[FA], rh.at[FA], (s, d - 1))

    def f_up():
        return remote(cf.at[pl.ds(ZD, RG)], cf.at[pl.ds(0, RG)], sh.at[FB], rh.at[FB], (s, d + 1))

    def home():
        @pl.when(cross_up)
        def _():
            for k in range(NSUB):
                over_up(k).start()

        @pl.when(cross_lo)
        def _():
            for k in range(NSUB):
                over_dn(k).start()

        for k in range(1, NSUB):
            back_out(k).start()
        cf[planes, c] = cs[s]
        for k in range(1, NSUB):
            back_in(k).wait_recv()

        @pl.when(near_lo)
        def _():
            f_dn().start()

        @pl.when(near_up)
        def _():
            f_up().start()

    def halo_drain():
        @pl.when(has_prev)
        def _():
            x_dn(core_p, XA, XA).wait_send()

        @pl.when(has_next)
        def _():
            x_up(core_p, XB, XB).wait_send()

        across_dn_x(lambda copy: copy.wait_send())
        across_up_x(lambda copy: copy.wait_send())

        @pl.when(has_lo)
        def _():
            z_dn(ext, ZA).wait_send()

        @pl.when(has_up)
        def _():
            z_up(ext, ZB).wait_send()

        @pl.when(near_lo)
        def _():
            i_dn().wait_send()
            i_up().wait_recv()

            @pl.when(has_prev)
            def _():
                z_dn(ext_top, CA0).wait_send()

            @pl.when(has_next)
            def _():
                z_dn(ext_bot, CA1).wait_send()

        @pl.when(near_up)
        def _():
            i_up().wait_send()
            i_dn().wait_recv()

            @pl.when(has_prev)
            def _():
                z_up(ext_top, CB0).wait_send()

            @pl.when(has_next)
            def _():
                z_up(ext_bot, CB1).wait_send()

    def slab_drain():
        def both(first):
            for k in range(1, NSUB):
                slab_out(k, first).wait_send()
                slab_in(k, first).wait_recv()

        @pl.when(cross_lo)
        def _():
            both(0)

        @pl.when(cross_up)
        def _():
            both(4)

    def spread_drain():
        for k in range(1, NSUB):
            chunk_out(k).wait_send()
            weight_out(k).wait_send()

    def home_drain():
        for k in range(1, NSUB):
            back_out(k).wait_send()

        @pl.when(cross_up)
        def _():
            for k in range(NSUB):
                over_up(k).wait_send()
                over_in(k, RG + ZD, d + 1).wait_recv()

        @pl.when(cross_lo)
        def _():
            for k in range(NSUB):
                over_dn(k).wait_send()
                over_in(k, 0, d - 1).wait_recv()

        @pl.when(near_lo)
        def _():
            f_dn().wait_send()
            f_up().wait_recv()

        @pl.when(near_up)
        def _():
            f_up().wait_send()
            f_dn().wait_recv()

    spread()
    halo_start()
    slabs()
    core_rows()
    corners_end()
    other_rows()
    boxes()
    combined()
    home()
    spread_drain()
    halo_drain()
    slab_drain()
    home_drain()


def smooth_kernel(cf, img, ih, vel, out, force):
    taps = gauss_taps()
    lane = lax.broadcasted_iota(jnp.int32, (X, Y), 1)
    row = lax.broadcasted_iota(jnp.int32, (X, Y), 0)
    comp = pl.program_id(0)

    def plane(i):
        if i < 4:
            return ih[i]
        if i < 4 + ZD:
            return img[i - 4]
        return ih[i - ZD]

    @pl.when(comp == 0)
    def _():
        for p in range(ZD + 2 * RG):
            force[p] = (cf[p] * 0.5) * (plane(p + 2) - plane(p))

    @pl.when(comp == 1)
    def _():
        for p in range(ZD + 2 * RG):
            here = plane(p + 1)
            below = jnp.where(row == X - 1, 0.0, pltpu.roll(here, X - 1, 0))
            above = jnp.where(row == 0, 0.0, pltpu.roll(here, 1, 0))
            force[p] = (cf[p] * 0.5) * (below - above)

    @pl.when(comp == 2)
    def _():
        for p in range(ZD + 2 * RG):
            here = plane(p + 1)
            after = jnp.where(lane == Y - 1, 0.0, pltpu.roll(here, Y - 1, 1))
            before = jnp.where(lane == 0, 0.0, pltpu.roll(here, 1, 1))
            force[p] = (cf[p] * 0.5) * (after - before)

    matrix = band(taps, jnp.float32)
    t_high = matrix.astype(jnp.bfloat16)
    t_low = (matrix - t_high.astype(jnp.float32)).astype(jnp.bfloat16)
    none = jnp.zeros((128, 128), jnp.bfloat16)
    right = jnp.concatenate(
        [jnp.concatenate([t_high, t_low], axis=1), jnp.concatenate([t_high, none], axis=1)], axis=0
    )
    left = jnp.concatenate(
        [jnp.concatenate([t_high, t_high], axis=1), jnp.concatenate([t_low, none], axis=1)], axis=0
    )

    def split(val):
        high = val.astype(jnp.bfloat16)
        return high, (val - high.astype(jnp.float32)).astype(jnp.bfloat16)

    for p in range(ZD):
        total = taps[RG] * force[p + RG]
        for k in range(1, RG + 1):
            total = total + taps[RG + k] * (force[p + RG - k] + force[p + RG + k])
        both = jnp.dot(jnp.concatenate(split(total), axis=1), right, preferred_element_type=jnp.float32)
        across = both[:, :Y] + both[:, Y:]
        both = jnp.dot(left, jnp.concatenate(split(across), axis=0), preferred_element_type=jnp.float32)
        out[0, p] = vel[0, p] + 40.0 * (both[:X] + both[X:])


def on_device(images, velocity, ref_index, ref_weights):
    vmem = pl.BlockSpec(memory_space=pltpu.VMEM)
    smem = pl.BlockSpec(memory_space=pltpu.SMEM)
    f32 = jnp.float32
    dma = pltpu.SemaphoreType.DMA
    cf, ih = pl.pallas_call(
        coeff_kernel,
        out_shape=(
            jax.ShapeDtypeStruct((ZD + 2 * RG, NSUB, ROWS, Y), f32),
            jax.ShapeDtypeStruct((8, NSUB, ROWS, Y), f32),
        ),
        in_specs=[smem, smem, pl.BlockSpec(memory_space=pltpu.HBM)],
        out_specs=(vmem, vmem),
        scratch_shapes=[
            pltpu.VMEM((ZD, NSUB, ROWS, Y), f32),
            pltpu.VMEM((NSUB, ZD, ROWS, Y), f32),
            pltpu.VMEM((NSUB, 8, 128), f32),
            pltpu.VMEM((ROWS, EXT_P, NSUB, Y), f32),
            pltpu.VMEM((RAD, EXT_P, NSUB, Y), f32),
            pltpu.VMEM((RAD, EXT_P, NSUB, Y), f32),
            pltpu.VMEM((NF, EXT_R, ZD, NSUB, Y), f32),
            pltpu.VMEM((NF * CELLS, NSUB, Y), f32),
            pltpu.VMEM((NF * CELLS, NSUB, Y), f32),
            pltpu.VMEM((CELLS, NSUB, Y), f32),
            pltpu.VMEM((CELLS, NSUB, Y), f32),
            pltpu.VMEM((CELLS * NSUB, Y), f32),
            pltpu.VMEM((NSUB, ZD, ROWS, Y), f32),
            pltpu.VMEM((NSUB, 4, ROWS, Y), f32),
            dma((NSUB,)), dma((NSUB,)), dma((NSUB,)), dma((NSUB,)), dma((NSUB,)),
            dma((NSUB,)), dma((NSUB,)), dma((NSUB,)), dma((NSUB,)), dma((NSUB,)),
            dma((14,)), dma((14,)), dma,
        ],
        compiler_params=pltpu.CompilerParams(
            collective_id=0, has_side_effects=True, vmem_limit_bytes=32 * 1024 * 1024
        ),
    )(ref_index, ref_weights, images.reshape(ZD, NSUB, ROWS, Y))
    out = pl.pallas_call(
        smooth_kernel,
        out_shape=jax.ShapeDtypeStruct((3, ZD, X, Y), f32),
        grid=(3,),
        in_specs=[vmem] * 3 + [pl.BlockSpec((1, ZD, X, Y), lambda i: (i, 0, 0, 0))],
        out_specs=pl.BlockSpec((1, ZD, X, Y), lambda i: (i, 0, 0, 0)),
        scratch_shapes=[pltpu.VMEM((ZD + 2 * RG, X, Y), f32)],
        compiler_params=pltpu.CompilerParams(vmem_limit_bytes=32 * 1024 * 1024),
    )(cf.reshape(ZD + 2 * RG, X, Y), images.reshape(ZD, X, Y), ih.reshape(8, X, Y), velocity.reshape(3, ZD, X, Y))
    return out.reshape(3, 1, ZD, X, Y)


def solution(mesh):
    placed = (
        P("subj", "depth", None, None),
        P(None, "subj", "depth", None, None),
        P(),
        P("subj", None),
    )
    return jax.shard_map(
        on_device,
        mesh=mesh,
        in_specs=placed,
        out_specs=P(None, "subj", "depth", None, None),
        check_vma=False,
    )
```

time: 66.1 us -> 57.9 us (0.88)
  the two profiles are of different devices: /device:TPU:56 before, /device:TPU:57 now
where the time goes in v2:
time: 57.9 us; the launch traced here: 57.8 us
  Pallas kernels  54.9 us (95%)
  local copies, waits for them, and re-layouts  2.84 us (5%)
    pallas_call x1, Pallas kernels, on_device(): pl.pallas_call(coeff_kernel, out_shape=(jax.ShapeDtypeStruct((ZD + 2 * RG...  51.2 us
    pallas_call x1, Pallas kernels, on_device(): pl.pallas_call(smooth_kernel, out_shape=jax.ShapeDtypeStruct((3, ZD, X, Y...  3.68 us
    unnamed x10, local copies, waits for them, and re-layouts  2.84 us

profile of v2, /device:TPU:57, one launch (start us, length us, event | category | flops | bytes accessed | tf_op | source)
XLA Modules:
  0.0 57.8 jit_solution(6846438942268773603)
XLA Ops:
  0.0 0.0 copy-start.3
  0.0 0.0 copy-start.4
  0.0 0.7 %copy-done.3 = s32[4]{0:T(128)S(1)} copy-done((s32[4]{0:T(128)S(1)}, s32[4]{0:T(128)}, u32[]{:S(2)}) %copy-start.3) | copy-done | bytes 40
  0.7 0.0 copy-done.4
  0.7 0.0 copy-start
  0.7 1.0 %copy-done = f32[1,5,128,128]{3,2,1,0:T(8,128)S(1)} copy-done((f32[1,5,128,128]{3,2,1,0:T(8,128)S(1)}, f32[1,5,128,128]{3,2,1,0:T(8,128)}, u32[]{:S(2)}) %copy-start) | copy-done | bytes 327704
  1.6 0.0 copy-start.1
  1.6 51.2 %shard_map.46 = (f32[11,16,8,128]{3,2,1,0:T(8,128)S(1)}, f32[8,16,8,128]{3,2,1,0:T(8,128)S(1)}) custom-call(s32[4]{0:T(128)S(1)} %copy-done.3, s32[1,4]{1,0:T(1,128)S(1)} %copy-done.4, f32[5,16,8,128]{3,2,1,0:T(8,128)S(1)} %bitcast.8), custom_call_target="tpu_custom_call" | custom-call | tf_op jit(solution)/shard_map/pallas_call | solution.py:654
  52.9 0.0 copy-done.1
  52.9 0.0 copy-start.2
  52.9 1.2 %copy-done.2 = f32[3,1,5,128,128]{4,3,2,1,0:T(8,128)S(1)} copy-done((f32[3,1,5,128,128]{4,3,2,1,0:T(8,128)S(1)}, f32[3,1,5,128,128]{4,3,2,1,0:T(8,128)}, u32[]{:S(2)}) %copy-start.2) | copy-done | bytes 983064
  54.1 3.7 %shard_map.47 = f32[3,5,128,128]{3,2,1,0:T(8,128)} custom-call(f32[11,128,128]{2,1,0:T(8,128)S(1)} %bitcast.11, f32[5,128,128]{2,1,0:T(8,128)S(1)} %bitcast.9, f32[8,128,128]{2,1,0:T(8,128)S(1)} %bitcast.12, f32[3,5,128,128]{3,2,1,0:T(8,128)S(1)} %bitcast.10), custom_call_target="tpu_custom_call" | custom-call | tf_op jit(solution)/shard_map/pallas_call | solution.py:685
Async XLA Ops:
  0.0 0.7 %copy-start.3 = (s32[4]{0:T(128)S(1)}, s32[4]{0:T(128)}, u32[]{:S(2)}) copy-start(s32[4]{0:T(128)} %idx_ref.1) | copy-start | bytes 52
  0.0 0.7 %copy-start.4 = (s32[1,4]{1,0:T(1,128)S(1)}, s32[1,4]{1,0:T(1,128)}, u32[]{:S(2)}) copy-start(s32[1,4]{1,0:T(1,128)} %w_ref.1) | copy-start | bytes 52
  0.7 1.0 %copy-start = (f32[1,5,128,128]{3,2,1,0:T(8,128)S(1)}, f32[1,5,128,128]{3,2,1,0:T(8,128)}, u32[]{:S(2)}) copy-start(f32[1,5,128,128]{3,2,1,0:T(8,128)} %param.4) | copy-start | bytes 983044
  1.6 51.2 %copy-start.1 = (f32[1,5,128,128]{3,2,1,0:T(8,128)S(1)}, f32[1,5,128,128]{3,2,1,0:T(8,128)}, u32[]{:S(2)}) copy-start(f32[1,5,128,128]{3,2,1,0:T(8,128)} %param.4) | copy-start | bytes 983044
  52.9 1.2 %copy-start.2 = (f32[3,1,5,128,128]{4,3,2,1,0:T(8,128)S(1)}, f32[3,1,5,128,128]{4,3,2,1,0:T(8,128)}, u32[]{:S(2)}) copy-start(f32[3,1,5,128,128]{4,3,2,1,0:T(8,128)} %param.5) | copy-start | bytes 2949124

commit v3 on v2

--- a/solution.py
+++ b/solution.py
@@ -22,9 +22,11 @@
 EXT_P = ZD + 2 * RAD
 CELLS = ROWS * ZD
 NF = 2 + NREF
+FP = ZD + 2 * RG
+VLIM = 32
 MESH = pl.DeviceIdType.MESH
 
-XA, XB, ZA, ZB, CA0, CA1, CB0, CB1, IA, IB, FA, FB, YA, YB = range(14)
+XA, XB, ZA, ZB, CA0, CA1, CB0, CB1, IA, IB, YA, YB, FA, FB = list(range(13)) + [16]
 
 
 def gauss_taps():
@@ -78,9 +80,9 @@
 
 
 def coeff_kernel(
-    idx_ref, w_ref, img_hbm, cf, ih,
-    img, a_buf, w_buf, ext, ext_top, ext_bot, zs, xs, bx, inv, dev, c_buf, cs, hs,
-    sa, ra, sw, rw, sr, rr, sg, rg, sc, rc, sh, rh, load_sem,
+    idx_ref, w_ref, img_hbm, out,
+    img, a_buf, w_buf, ext, ext_top, ext_bot, zs, xs, bx, inv, dev, c_buf, cs, b_buf, cf, ih, grad, part,
+    sa, ra, sw, rw, sr, rr, sb, rb, sg, rg, sc, rc, sh, rh, load_sem,
 ):
     s = lax.axis_index("subj")
     d = lax.axis_index("depth")
@@ -88,14 +90,10 @@
     half = nd // 2
     hi = d // half
     c = chunk_of(s, hi)
-    mirror = 4 * (3 - s // 4) + s % 4
     has_lo, has_up = d > 0, d < nd - 1
     cross_lo, cross_up = d == half, d == half - 1
     near_lo, near_up = has_lo & (d != half), has_up & (d != half - 1)
     has_prev, has_next = c > 0, c < NSUB - 1
-    s_lo = jnp.where(cross_lo, mirror, s)
-    s_up = jnp.where(cross_up, mirror, s)
-
     load = pltpu.make_async_copy(img_hbm, img, load_sem)
     load.start()
 
@@ -182,11 +180,27 @@
         frm = peer_from(k)
         return remote(w_buf.at[frm], w_buf.at[frm], sw.at[k], rw.at[frm], (frm, d))
 
+    def far_out(k, first, side):
+        to = peer_to(k)
+        return remote(img.at[pl.ds(first, 4), chunk_of(to, 1 - hi)], b_buf.at[s], sb.at[k], rb.at[s], (to, side))
+
+    def far_in(k, side):
+        return remote(b_buf.at[k], b_buf.at[k], sb.at[k], rb.at[k], (s, side))
+
     def spread():
         for k in range(1, NSUB):
             chunk_out(k).start()
-        for k in range(1, NSUB):
-            weight_out(k).start()
+
+        @pl.when(cross_up)
+        def _():
+            for k in range(NSUB):
+                far_out(k, 1, d + 1).start()
+
+        @pl.when(cross_lo)
+        def _():
+            for k in range(NSUB):
+                far_out(k, 0, d - 1).start()
+
         a_buf[s] = img[:, c]
         for k in range(1, NSUB):
             chunk_in(k).wait_recv()
@@ -206,10 +220,10 @@
         return remote(ext.at[pl.ds(RAD, RAD), planes], ext_top.at[:, planes], sh.at[send], rh.at[recv], (nxt, d))
 
     def z_dn(block, sem):
-        return remote(block.at[:, pl.ds(RAD, RAD)], block.at[:, high_p], sh.at[sem], rh.at[sem], (s_lo, d - 1))
+        return remote(block.at[:, pl.ds(RAD, RAD)], block.at[:, high_p], sh.at[sem], rh.at[sem], (s, d - 1))
 
     def z_up(block, sem):
-        return remote(block.at[:, pl.ds(ZD, RAD)], block.at[:, low_p], sh.at[sem], rh.at[sem], (s_up, d + 1))
+        return remote(block.at[:, pl.ds(ZD, RAD)], block.at[:, low_p], sh.at[sem], rh.at[sem], (s, d + 1))
 
     def i_dn():
         return remote(img.at[pl.ds(0, 4)], ih.at[pl.ds(4, 4)], sh.at[IA], rh.at[IA], (s, d - 1))
@@ -240,11 +254,11 @@
                 go(x_up(low_p, YB, CB0))
 
     def halo_start():
-        @pl.when(has_lo)
+        @pl.when(near_lo)
         def _():
             z_dn(ext, ZA).start()
 
-        @pl.when(has_up)
+        @pl.when(near_up)
         def _():
             z_up(ext, ZB).start()
 
@@ -256,6 +270,9 @@
         def _():
             x_up(core_p, XB, XB).start()
 
+        for k in range(1, NSUB):
+            weight_out(k).start()
+
         @pl.when(has_next)
         def _():
             x_dn(core_p, XA, XA).wait_recv()
@@ -280,53 +297,64 @@
             def _():
                 z_up(ext_top, CB0).start()
 
-        @pl.when(has_up)
-        def _():
-            z_dn(ext, ZA).wait_recv()
-
-        @pl.when(has_lo)
-        def _():
-            z_up(ext, ZB).wait_recv()
+        b_flat = b_buf.reshape(NSUB * 4 * ROWS, Y)
+
+        def far_end(side, base):
+            for k in range(NSUB):
+                far_in(k, side).wait_recv()
+            for p in range(4):
+                for r in range(ROWS):
+                    ext[r, base + p] = b_flat[pl.ds(p * ROWS + r, NSUB, stride=4 * ROWS), :]
+
+        @pl.when(cross_lo)
+        def _():
+            far_end(d - 1, 0)
+
+        @pl.when(cross_up)
+        def _():
+            far_end(d + 1, RAD + ZD)
 
         across_dn_x(lambda copy: copy.start())
         across_up_x(lambda copy: copy.start())
 
+        @pl.when(near_up)
+        def _():
+            z_dn(ext, ZA).wait_recv()
+
         @pl.when(near_lo)
         def _():
+            z_up(ext, ZB).wait_recv()
+
+        @pl.when(near_lo)
+        def _():
             i_dn().start()
 
         @pl.when(near_up)
         def _():
             i_up().start()
-
-    e_flat = ext.reshape(ROWS * EXT_P * NSUB, Y)
 
     def slab_out(k, first):
         to = peer_to(k)
-        return remote(hs.at[to], ih.at[pl.ds(first, 4), c], sg.at[k], rg.at[c], (to, d))
+        return remote(b_buf.at[to], ih.at[pl.ds(first, 4), c], sg.at[k], rg.at[c], (to, d))
 
     def slab_in(k, first):
         frm = peer_from(k)
         chunk = chunk_of(frm, hi)
-        return remote(hs.at[frm], ih.at[pl.ds(first, 4), chunk], sg.at[k], rg.at[chunk], (frm, d))
-
-    def slab_start(base, first):
-        for sub in range(NSUB):
-            for p in range(4):
-                at = (base + p) * NSUB + sub
-                hs[sub, p] = e_flat[pl.ds(at, ROWS, stride=EXT_P * NSUB), :]
+        return remote(b_buf.at[frm], ih.at[pl.ds(first, 4), chunk], sg.at[k], rg.at[chunk], (frm, d))
+
+    def slab_start(first):
         for k in range(1, NSUB):
             slab_out(k, first).start()
-        ih[pl.ds(first, 4), c] = hs[s]
+        ih[pl.ds(first, 4), c] = b_buf[s]
 
     def slabs():
         @pl.when(cross_lo)
         def _():
-            slab_start(0, 0)
-
-        @pl.when(cross_up)
-        def _():
-            slab_start(RAD + ZD, 4)
+            slab_start(0)
+
+        @pl.when(cross_up)
+        def _():
+            slab_start(4)
 
     def corners_end():
         @pl.when(has_up)
@@ -430,14 +458,17 @@
 
     planes = pl.ds(RG, ZD)
 
-    def back_out(k):
-        to = peer_to(k)
-        return remote(cs.at[to], cf.at[planes, c], sr.at[k], rr.at[c], (to, d))
-
-    def back_in(k):
-        frm = peer_from(k)
+    y_at, x_at = s // 4, s % 4
+    pairs = [(j, i) for j in range(4) for i in range(4) if (j, i) != (0, 0)]
+
+    def back_out(j, i):
+        to = 4 * ((y_at + j) % 4) + (x_at + i) % 4
+        return remote(cs.at[to], cf.at[planes, c], sr.at[4 * j + i], rr.at[c], (to, d))
+
+    def back_in(j, i):
+        frm = 4 * ((y_at + 4 - j) % 4) + (x_at + 4 - i) % 4
         chunk = chunk_of(frm, hi)
-        return remote(cs.at[frm], cf.at[planes, chunk], sr.at[k], rr.at[chunk], (frm, d))
+        return remote(cs.at[frm], cf.at[planes, chunk], sr.at[4 * j + i], rr.at[chunk], (frm, d))
 
     def over_up(k):
         to = peer_to(k)
@@ -450,13 +481,18 @@
     def over_in(k, first, side):
         return remote(cs.at[k, pl.ds(0, RG)], cf.at[pl.ds(first, RG), k], sc.at[k], rc.at[k], (s, side))
 
-    def f_dn():
-        return remote(cf.at[pl.ds(RG, RG)], cf.at[pl.ds(RG + ZD, RG)], sh.at[FA], rh.at[FA], (s, d - 1))
-
-    def f_up():
-        return remote(cf.at[pl.ds(ZD, RG)], cf.at[pl.ds(0, RG)], sh.at[FB], rh.at[FB], (s, d + 1))
-
-    def home():
+    def four(j):
+        return pl.ds(chunk_of(4 * ((y_at + 4 - j) % 4), hi) // 4 * 4, 4)
+
+    def f_dn(j):
+        return remote(
+            cf.at[pl.ds(RG, RG), four(j)], cf.at[pl.ds(RG + ZD, RG), four(j)], sh.at[FA + j], rh.at[FA + j], (s, d - 1)
+        )
+
+    def f_up(j):
+        return remote(cf.at[pl.ds(ZD, RG), four(j)], cf.at[pl.ds(0, RG), four(j)], sh.at[FB + j], rh.at[FB + j], (s, d + 1))
+
+    def home_start():
         @pl.when(cross_up)
         def _():
             for k in range(NSUB):
@@ -467,19 +503,127 @@
             for k in range(NSUB):
                 over_dn(k).start()
 
-        for k in range(1, NSUB):
-            back_out(k).start()
+        for j, i in pairs:
+            back_out(j, i).start()
         cf[planes, c] = cs[s]
-        for k in range(1, NSUB):
-            back_in(k).wait_recv()
-
+
+    def home_end():
+        for j in range(4):
+            for i in range(4):
+                if (j, i) != (0, 0):
+                    back_in(j, i).wait_recv()
+
+            @pl.when(near_lo)
+            def _():
+                f_dn(j).start()
+
+            @pl.when(near_up)
+            def _():
+                f_up(j).start()
+
+    taps = gauss_taps()
+    lane = lax.broadcasted_iota(jnp.int32, (X, Y), 1)
+    line = lax.broadcasted_iota(jnp.int32, (X, Y), 0)
+
+    def plane(i):
+        if i < 4:
+            return ih[i].reshape(X, Y)
+        if i < 4 + ZD:
+            return img[i - 4].reshape(X, Y)
+        return ih[i - ZD].reshape(X, Y)
+
+    def gradients():
         @pl.when(near_lo)
         def _():
-            f_dn().start()
+            i_up().wait_recv()
 
         @pl.when(near_up)
         def _():
-            f_up().start()
+            i_dn().wait_recv()
+
+        @pl.when(cross_lo)
+        def _():
+            for k in range(1, NSUB):
+                slab_in(k, 0).wait_recv()
+
+        @pl.when(cross_up)
+        def _():
+            for k in range(1, NSUB):
+                slab_in(k, 4).wait_recv()
+
+        for p in range(FP):
+            here = plane(p + 1)
+            grad[0, p] = (plane(p + 2) - plane(p)) * 0.5
+            below = jnp.where(line == X - 1, 0.0, pltpu.roll(here, X - 1, 0))
+            above = jnp.where(line == 0, 0.0, pltpu.roll(here, 1, 0))
+            grad[1, p] = (below - above) * 0.5
+            after = jnp.where(lane == Y - 1, 0.0, pltpu.roll(here, Y - 1, 1))
+            before = jnp.where(lane == 0, 0.0, pltpu.roll(here, 1, 1))
+            grad[2, p] = (after - before) * 0.5
+
+    def depth_sum(comp, p, inner):
+        total = None
+        for k in range(2 * RG + 1):
+            q = p + k
+            if (RG <= q < RG + ZD) == inner:
+                term = (taps[k] * cf[q].reshape(X, Y)) * grad[comp, q]
+                total = term if total is None else total + term
+        return total
+
+    def inner_part():
+        def body(comp, carry):
+            for p in range(ZD):
+                part[comp, p] = depth_sum(comp, p, True)
+            return carry
+
+        lax.fori_loop(0, 3, body, 0)
+
+    def halo_part():
+        @pl.when(near_lo)
+        def _():
+            for j in range(4):
+                f_up(j).wait_recv()
+
+        @pl.when(near_up)
+        def _():
+            for j in range(4):
+                f_dn(j).wait_recv()
+
+        @pl.when(cross_up)
+        def _():
+            for k in range(NSUB):
+                over_in(k, RG + ZD, d + 1).wait_recv()
+
+        @pl.when(cross_lo)
+        def _():
+            for k in range(NSUB):
+                over_in(k, 0, d - 1).wait_recv()
+
+        matrix = band(taps, jnp.float32)
+        t_high = matrix.astype(jnp.bfloat16)
+        t_low = (matrix - t_high.astype(jnp.float32)).astype(jnp.bfloat16)
+        none = jnp.zeros((128, 128), jnp.bfloat16)
+        right = jnp.concatenate(
+            [jnp.concatenate([t_high, t_low], axis=1), jnp.concatenate([t_high, none], axis=1)], axis=0
+        )
+        left = jnp.concatenate(
+            [jnp.concatenate([t_high, t_high], axis=1), jnp.concatenate([t_low, none], axis=1)], axis=0
+        )
+
+        def split(val):
+            high = val.astype(jnp.bfloat16)
+            return high, (val - high.astype(jnp.float32)).astype(jnp.bfloat16)
+
+        def body(comp, carry):
+            for p in range(ZD):
+                total = part[comp, p] + depth_sum(comp, p, False)
+                both = jnp.dot(jnp.concatenate(split(total), axis=1), right, preferred_element_type=jnp.float32)
+                across = both[:, :Y] + both[:, Y:]
+                both = jnp.dot(left, jnp.concatenate(split(across), axis=0), preferred_element_type=jnp.float32)
+                out[comp, p] = 40.0 * (both[:X] + both[X:])
+            return carry
+
+        lax.fori_loop(0, 3, body, 0)
 
     def halo_drain():
         @pl.when(has_prev)
@@ -493,31 +637,23 @@
         across_dn_x(lambda copy: copy.wait_send())
         across_up_x(lambda copy: copy.wait_send())
 
-        @pl.when(has_lo)
-        def _():
+        @pl.when(near_lo)
+        def _():
+            i_dn().wait_send()
             z_dn(ext, ZA).wait_send()
 
-        @pl.when(has_up)
-        def _():
+            @pl.when(has_prev)
+            def _():
+                z_dn(ext_top, CA0).wait_send()
+
+            @pl.when(has_next)
+            def _():
+                z_dn(ext_bot, CA1).wait_send()
+
+        @pl.when(near_up)
+        def _():
+            i_up().wait_send()
             z_up(ext, ZB).wait_send()
-
-        @pl.when(near_lo)
-        def _():
-            i_dn().wait_send()
-            i_up().wait_recv()
-
-            @pl.when(has_prev)
-            def _():
-                z_dn(ext_top, CA0).wait_send()
-
-            @pl.when(has_next)
-            def _():
-                z_dn(ext_bot, CA1).wait_send()
-
-        @pl.when(near_up)
-        def _():
-            i_up().wait_send()
-            i_dn().wait_recv()
 
             @pl.when(has_prev)
             def _():
@@ -531,7 +667,6 @@
         def both(first):
             for k in range(1, NSUB):
                 slab_out(k, first).wait_send()
-                slab_in(k, first).wait_recv()
 
         @pl.when(cross_lo)
         def _():
@@ -546,31 +681,39 @@
             chunk_out(k).wait_send()
             weight_out(k).wait_send()
 
+        @pl.when(cross_up)
+        def _():
+            for k in range(NSUB):
+                far_out(k, 1, d + 1).wait_send()
+
+        @pl.when(cross_lo)
+        def _():
+            for k in range(NSUB):
+                far_out(k, 0, d - 1).wait_send()
+
     def home_drain():
-        for k in range(1, NSUB):
-            back_out(k).wait_send()
+        for j, i in pairs:
+            back_out(j, i).wait_send()
 
         @pl.when(cross_up)
         def _():
             for k in range(NSUB):
                 over_up(k).wait_send()
-                over_in(k, RG + ZD, d + 1).wait_recv()
 
         @pl.when(cross_lo)
         def _():
             for k in range(NSUB):
                 over_dn(k).wait_send()
-                over_in(k, 0, d - 1).wait_recv()
 
         @pl.when(near_lo)
         def _():
-            f_dn().wait_send()
-            f_up().wait_recv()
+            for j in range(4):
+                f_dn(j).wait_send()
 
         @pl.when(near_up)
         def _():
-            f_up().wait_send()
-            f_dn().wait_recv()
+            for j in range(4):
+                f_up(j).wait_send()
 
     spread()
     halo_start()
@@ -580,70 +723,15 @@
     other_rows()
     boxes()
     combined()
-    home()
+    home_start()
+    gradients()
     spread_drain()
     halo_drain()
     slab_drain()
+    home_end()
+    inner_part()
+    halo_part()
     home_drain()
-
-
-def smooth_kernel(cf, img, ih, vel, out, force):
-    taps = gauss_taps()
-    lane = lax.broadcasted_iota(jnp.int32, (X, Y), 1)
-    row = lax.broadcasted_iota(jnp.int32, (X, Y), 0)
-    comp = pl.program_id(0)
-
-    def plane(i):
-        if i < 4:
-            return ih[i]
-        if i < 4 + ZD:
-            return img[i - 4]
-        return ih[i - ZD]
-
-    @pl.when(comp == 0)
-    def _():
-        for p in range(ZD + 2 * RG):
-            force[p] = (cf[p] * 0.5) * (plane(p + 2) - plane(p))
-
-    @pl.when(comp == 1)
-    def _():
-        for p in range(ZD + 2 * RG):
-            here = plane(p + 1)
-            below = jnp.where(row == X - 1, 0.0, pltpu.roll(here, X - 1, 0))
-            above = jnp.where(row == 0, 0.0, pltpu.roll(here, 1, 0))
-            force[p] = (cf[p] * 0.5) * (below - above)
-
-    @pl.when(comp == 2)
-    def _():
-        for p in range(ZD + 2 * RG):
-            here = plane(p + 1)
-            after = jnp.where(lane == Y - 1, 0.0, pltpu.roll(here, Y - 1, 1))
-            before = jnp.where(lane == 0, 0.0, pltpu.roll(here, 1, 1))
-            force[p] = (cf[p] * 0.5) * (after - before)
-
-    matrix = band(taps, jnp.float32)
-    t_high = matrix.astype(jnp.bfloat16)
-    t_low = (matrix - t_high.astype(jnp.float32)).astype(jnp.bfloat16)
-    none = jnp.zeros((128, 128), jnp.bfloat16)
-    right = jnp.concatenate(
-        [jnp.concatenate([t_high, t_low], axis=1), jnp.concatenate([t_high, none], axis=1)], axis=0
-    )
-    left = jnp.concatenate(
-        [jnp.concatenate([t_high, t_high], axis=1), jnp.concatenate([t_low, none], axis=1)], axis=0
-    )
-
-    def split(val):
-        high = val.astype(jnp.bfloat16)
-        return high, (val - high.astype(jnp.float32)).astype(jnp.bfloat16)
-
-    for p in range(ZD):
-        total = taps[RG] * force[p + RG]
-        for k in range(1, RG + 1):
-            total = total + taps[RG + k] * (force[p + RG - k] + force[p + RG + k])
-        both = jnp.dot(jnp.concatenate(split(total), axis=1), right, preferred_element_type=jnp.float32)
-        across = both[:, :Y] + both[:, Y:]
-        both = jnp.dot(left, jnp.concatenate(split(across), axis=0), preferred_element_type=jnp.float32)
-        out[0, p] = vel[0, p] + 40.0 * (both[:X] + both[X:])
 
 
 def on_device(images, velocity, ref_index, ref_weights):
@@ -651,14 +739,11 @@
     smem = pl.BlockSpec(memory_space=pltpu.SMEM)
     f32 = jnp.float32
     dma = pltpu.SemaphoreType.DMA
-    cf, ih = pl.pallas_call(
+    smooth = pl.pallas_call(
         coeff_kernel,
-        out_shape=(
-            jax.ShapeDtypeStruct((ZD + 2 * RG, NSUB, ROWS, Y), f32),
-            jax.ShapeDtypeStruct((8, NSUB, ROWS, Y), f32),
-        ),
+        out_shape=jax.ShapeDtypeStruct((3, ZD, X, Y), f32),
         in_specs=[smem, smem, pl.BlockSpec(memory_space=pltpu.HBM)],
-        out_specs=(vmem, vmem),
+        out_specs=vmem,
         scratch_shapes=[
             pltpu.VMEM((ZD, NSUB, ROWS, Y), f32),
             pltpu.VMEM((NSUB, ZD, ROWS, Y), f32),
@@ -674,24 +759,19 @@
             pltpu.VMEM((CELLS * NSUB, Y), f32),
             pltpu.VMEM((NSUB, ZD, ROWS, Y), f32),
             pltpu.VMEM((NSUB, 4, ROWS, Y), f32),
-            dma((NSUB,)), dma((NSUB,)), dma((NSUB,)), dma((NSUB,)), dma((NSUB,)),
-            dma((NSUB,)), dma((NSUB,)), dma((NSUB,)), dma((NSUB,)), dma((NSUB,)),
-            dma((14,)), dma((14,)), dma,
+            pltpu.VMEM((FP, NSUB, ROWS, Y), f32),
+            pltpu.VMEM((8, NSUB, ROWS, Y), f32),
+            pltpu.VMEM((3, FP, X, Y), f32),
+            pltpu.VMEM((3, ZD, X, Y), f32),
+            dma((NSUB,)), dma((NSUB,)), dma((NSUB,)), dma((NSUB,)), dma((NSUB,)), dma((NSUB,)),
+            dma((NSUB,)), dma((NSUB,)), dma((NSUB,)), dma((NSUB,)), dma((NSUB,)), dma((NSUB,)),
+            dma((20,)), dma((20,)), dma,
         ],
         compiler_params=pltpu.CompilerParams(
-            collective_id=0, has_side_effects=True, vmem_limit_bytes=32 * 1024 * 1024
+            collective_id=0, has_side_effects=True, vmem_limit_bytes=VLIM * 1024 * 1024
         ),
     )(ref_index, ref_weights, images.reshape(ZD, NSUB, ROWS, Y))
-    out = pl.pallas_call(
-        smooth_kernel,
-        out_shape=jax.ShapeDtypeStruct((3, ZD, X, Y), f32),
-        grid=(3,),
-        in_specs=[vmem] * 3 + [pl.BlockSpec((1, ZD, X, Y), lambda i: (i, 0, 0, 0))],
-        out_specs=pl.BlockSpec((1, ZD, X, Y), lambda i: (i, 0, 0, 0)),
-        scratch_shapes=[pltpu.VMEM((ZD + 2 * RG, X, Y), f32)],
-        compiler_params=pltpu.CompilerParams(vmem_limit_bytes=32 * 1024 * 1024),
-    )(cf.reshape(ZD + 2 * RG, X, Y), images.reshape(ZD, X, Y), ih.reshape(8, X, Y), velocity.reshape(3, ZD, X, Y))
-    return out.reshape(3, 1, ZD, X, Y)
+    return velocity + smooth.reshape(3, 1, ZD, X, Y)
 
 
 def solution(mesh):

time: 57.9 us -> 54.8 us (0.946)
  the two profiles are of different devices: /device:TPU:57 before, /device:TPU:40 now
where the time goes in v3:
time: 54.8 us; the launch traced here: 54.6 us
  Pallas kernels  51.9 us (95%)
  local copies, waits for them, and re-layouts  1.65 us (3%)
  other arithmetic  1.05 us (2%)
    pallas_call x1, Pallas kernels, on_device(): pl.pallas_call(coeff_kernel, out_shape=jax.ShapeDtypeStruct((3, ZD, X, Y)...  51.9 us
    unnamed x8, local copies, waits for them, and re-layouts  1.65 us

profile of v3, /device:TPU:40, one launch (start us, length us, event | category | flops | bytes accessed | tf_op | source)
XLA Modules:
  0.0 54.6 jit_solution(12133697044752726469)
XLA Ops:
  0.0 0.0 copy-start.2
  0.0 0.0 copy-start.1
  0.0 0.7 %copy-done.2 = s32[1,4]{1,0:T(1,128)S(1)} copy-done((s32[1,4]{1,0:T(1,128)S(1)}, s32[1,4]{1,0:T(1,128)}, u32[]{:S(2)}) %copy-start.2) | copy-done | bytes 40
  0.7 0.0 copy-done.1
  0.7 0.0 copy-start
  0.7 1.0 %copy-done = f32[1,5,128,128]{3,2,1,0:T(8,128)S(1)} copy-done((f32[1,5,128,128]{3,2,1,0:T(8,128)S(1)}, f32[1,5,128,128]{3,2,1,0:T(8,128)}, u32[]{:S(2)}) %copy-start) | copy-done | bytes 327704
  1.6 0.0 copy-start.3
  1.6 51.9 %shard_map.46 = f32[3,5,128,128]{3,2,1,0:T(8,128)S(1)} custom-call(s32[4]{0:T(128)S(1)} %copy-done.1, s32[1,4]{1,0:T(1,128)S(1)} %copy-done.2, f32[5,16,8,128]{3,2,1,0:T(8,128)S(1)} %bitcast.9), custom_call_target="tpu_custom_call" | custom-call | tf_op jit(solution)/shard_map/pallas_call | solution.py:742
  53.6 0.0 copy-done.3
  53.6 1.1 %fusion = f32[3,1,5,128,128]{4,3,2,1,0:T(8,128)} fusion(f32[3,5,128,128]{3,2,1,0:T(8,128)S(1)} %shard_map.46, f32[3,1,5,128,128]{4,3,2,1,0:T(8,128)S(1)} %copy-done.3), kind=kLoop, calls=%fused_computation.1 | loop fusion | flops 245760 | bytes 2949120 | tf_op jit(solution)/shard_map/add | solution.py:774
Async XLA Ops:
  0.0 0.7 %copy-start.2 = (s32[1,4]{1,0:T(1,128)S(1)}, s32[1,4]{1,0:T(1,128)}, u32[]{:S(2)}) copy-start(s32[1,4]{1,0:T(1,128)} %w_ref.1) | copy-start | bytes 52
  0.0 0.7 %copy-start.1 = (s32[4]{0:T(128)S(1)}, s32[4]{0:T(128)}, u32[]{:S(2)}) copy-start(s32[4]{0:T(128)} %idx_ref.1) | copy-start | bytes 52
  0.7 1.0 %copy-start = (f32[1,5,128,128]{3,2,1,0:T(8,128)S(1)}, f32[1,5,128,128]{3,2,1,0:T(8,128)}, u32[]{:S(2)}) copy-start(f32[1,5,128,128]{3,2,1,0:T(8,128)} %param.4) | copy-start | bytes 983044
  1.6 51.9 %copy-start.3 = (f32[3,1,5,128,128]{4,3,2,1,0:T(8,128)S(1)}, f32[3,1,5,128,128]{4,3,2,1,0:T(8,128)}, u32[]{:S(2)}) copy-start(f32[3,1,5,128,128]{4,3,2,1,0:T(8,128)} %param.5) | copy-start | bytes 2949124

commit v4 on v3

--- a/solution.py
+++ b/solution.py
@@ -392,10 +392,14 @@
                 zs[2 + r, at, k] = total
         return carry
 
-    def row_pass(f, carry):
-        for k in range(ZD):
-            for r, total in enumerate(window_rows([zs[f, row, k] for row in range(EXT_R)])):
-                xs[f * CELLS + r * ZD + k] = total
+    odd = d % 2
+    parts = ((2 * odd, 3), (3 - 3 * odd, 2))
+
+    def row_pass(base, n, f, carry):
+        for k in range(n):
+            at = base + k
+            for r, total in enumerate(window_rows([zs[f, row, at] for row in range(EXT_R)])):
+                xs[(f * ZD + at) * ROWS + r] = total
         return carry
 
     def core_rows():
@@ -405,42 +409,42 @@
         lax.fori_loop(0, RAD, functools.partial(depth_pass, ext_top, 0), 0)
         lax.fori_loop(0, RAD, functools.partial(depth_pass, ext_bot, RAD + ROWS), 0)
 
-    def boxes():
-        lax.fori_loop(0, NF, row_pass, 0)
+    def boxes(base, n):
+        lax.fori_loop(0, NF, functools.partial(row_pass, base, n), 0)
         ones = band([1.0] * WIN, jnp.bfloat16)
         ones2 = jnp.concatenate([ones, ones], axis=0)
-
-        def lane_pass(b, carry):
-            val = xs[pl.ds(b * 20, 20)].reshape(320, Y)
+        size = n * ROWS
+
+        def lane_pass(f, carry):
+            block = pl.ds((f * ZD + base) * ROWS, size)
+            val = xs[block].reshape(size * NSUB, Y)
             high = val.astype(jnp.bfloat16)
             rest = val - high.astype(jnp.float32)
             mid = rest.astype(jnp.bfloat16)
             low = (rest - mid.astype(jnp.float32)).astype(jnp.bfloat16)
             total = jnp.dot(jnp.concatenate([high, mid], axis=1), ones2, preferred_element_type=jnp.float32)
             total = total + jnp.dot(low, ones, preferred_element_type=jnp.float32)
-            bx[pl.ds(b * 20, 20)] = (total * (1.0 / WIN**3)).reshape(20, NSUB, Y)
+            bx[block] = (total * (1.0 / WIN**3)).reshape(size, NSUB, Y)
             return carry
 
-        lax.fori_loop(0, NF * CELLS // 20, lane_pass, 0)
-
-    def combined():
+        lax.fori_loop(0, NF, lane_pass, 0)
+
+    def combined(base, n):
         def stats(r, carry):
-            for k in range(ZD):
-                q = r * ZD + k
+            for k in range(n):
+                q = (base + k) * ROWS + r
                 mean = bx[q]
                 inv[q] = 1.0 / (bx[CELLS + q] - mean * mean + 1e-5)
-                dev[q] = ext[r, RAD + k] - mean
+                dev[q] = ext[r, RAD + base + k] - mean
             return carry
 
         lax.fori_loop(0, ROWS, stats, 0)
-        for k in range(1, NSUB):
-            weight_in(k).wait_recv()
         w_flat = w_buf.reshape(NSUB * 8, 128)
         weights = [w_flat[pl.ds(r, NSUB, stride=8), :] for r in range(NREF)]
 
         def combine(row, carry):
-            for k in range(ZD):
-                q = row * ZD + k
+            for k in range(n):
+                q = (base + k) * ROWS + row
                 mean_i, inv_i, dev_i = bx[q], inv[q], dev[q]
                 total = None
                 for r in range(NREF):
@@ -448,27 +452,38 @@
                     gain = (bx[(2 + r) * CELLS + q] - mean_i * bx[q, one, :]) * inv_i
                     term = (2.0 * gain * inv[q, one, :]) * (dev[q, one, :] - gain * dev_i) * weights[r]
                     total = term if total is None else total + term
-                c_buf[pl.ds(q * NSUB, NSUB), :] = total
+                c_buf[pl.ds((k * ROWS + row) * NSUB, NSUB), :] = total
             return carry
 
         lax.fori_loop(0, ROWS, combine, 0)
         for sub in range(NSUB):
-            for p in range(ZD):
-                cs[sub, p] = c_buf[pl.ds(p * NSUB + sub, ROWS, stride=ZD * NSUB), :]
-
-    planes = pl.ds(RG, ZD)
+            for k in range(n):
+                cs[sub, base + k] = c_buf[pl.ds(k * ROWS * NSUB + sub, ROWS, stride=NSUB), :]
+
+    def weights_end():
+        for k in range(1, NSUB):
+            weight_in(k).wait_recv()
+
 
     y_at, x_at = s // 4, s % 4
     pairs = [(j, i) for j in range(4) for i in range(4) if (j, i) != (0, 0)]
 
-    def back_out(j, i):
+    def back_out(j, i, part):
         to = 4 * ((y_at + j) % 4) + (x_at + i) % 4
-        return remote(cs.at[to], cf.at[planes, c], sr.at[4 * j + i], rr.at[c], (to, d))
-
-    def back_in(j, i):
+        base, n = parts[part]
+        sem = part * NSUB + 4 * j + i
+        return remote(
+            cs.at[to, pl.ds(base, n)], cf.at[pl.ds(RG + base, n), c], sr.at[sem], rr.at[part * NSUB + c], (to, d)
+        )
+
+    def back_in(j, i, part):
         frm = 4 * ((y_at + 4 - j) % 4) + (x_at + 4 - i) % 4
         chunk = chunk_of(frm, hi)
-        return remote(cs.at[frm], cf.at[planes, chunk], sr.at[4 * j + i], rr.at[chunk], (frm, d))
+        base, n = parts[part]
+        sem = part * NSUB + 4 * j + i
+        return remote(
+            cs.at[frm, pl.ds(base, n)], cf.at[pl.ds(RG + base, n), chunk], sr.at[sem], rr.at[part * NSUB + chunk], (frm, d)
+        )
 
     def over_up(k):
         to = peer_to(k)
@@ -492,32 +507,34 @@
     def f_up(j):
         return remote(cf.at[pl.ds(ZD, RG), four(j)], cf.at[pl.ds(0, RG), four(j)], sh.at[FB + j], rh.at[FB + j], (s, d + 1))
 
-    def home_start():
-        @pl.when(cross_up)
-        def _():
-            for k in range(NSUB):
-                over_up(k).start()
-
-        @pl.when(cross_lo)
-        def _():
-            for k in range(NSUB):
-                over_dn(k).start()
+    def home_start(part):
+        if part == 0:
+            @pl.when(cross_up)
+            def _():
+                for k in range(NSUB):
+                    over_up(k).start()
+
+            @pl.when(cross_lo)
+            def _():
+                for k in range(NSUB):
+                    over_dn(k).start()
 
         for j, i in pairs:
-            back_out(j, i).start()
-        cf[planes, c] = cs[s]
-
-    def home_end():
+            back_out(j, i, part).start()
+        base, n = parts[part]
+        cf[pl.ds(RG + base, n), c] = cs[s, pl.ds(base, n)]
+
+    def home_end(part):
         for j in range(4):
             for i in range(4):
                 if (j, i) != (0, 0):
-                    back_in(j, i).wait_recv()
-
-            @pl.when(near_lo)
+                    back_in(j, i, part).wait_recv()
+
+            @pl.when(near_lo & (odd == part))
             def _():
                 f_dn(j).start()
 
-            @pl.when(near_up)
+            @pl.when(near_up & (odd == 1 - part))
             def _():
                 f_up(j).start()
 
@@ -693,7 +710,8 @@
 
     def home_drain():
         for j, i in pairs:
-            back_out(j, i).wait_send()
+            back_out(j, i, 0).wait_send()
+            back_out(j, i, 1).wait_send()
 
         @pl.when(cross_up)
         def _():
@@ -721,14 +739,17 @@
     core_rows()
     corners_end()
     other_rows()
-    boxes()
-    combined()
-    home_start()
+    weights_end()
+    for turn in range(2):
+        boxes(*parts[turn])
+        combined(*parts[turn])
+        home_start(turn)
     gradients()
     spread_drain()
     halo_drain()
     slab_drain()
-    home_end()
+    home_end(0)
+    home_end(1)
     inner_part()
     halo_part()
     home_drain()
@@ -763,14 +784,14 @@
             pltpu.VMEM((8, NSUB, ROWS, Y), f32),
             pltpu.VMEM((3, FP, X, Y), f32),
             pltpu.VMEM((3, ZD, X, Y), f32),
-            dma((NSUB,)), dma((NSUB,)), dma((NSUB,)), dma((NSUB,)), dma((NSUB,)), dma((NSUB,)),
+            dma((NSUB,)), dma((NSUB,)), dma((NSUB,)), dma((NSUB,)), dma((2 * NSUB,)), dma((2 * NSUB,)),
             dma((NSUB,)), dma((NSUB,)), dma((NSUB,)), dma((NSUB,)), dma((NSUB,)), dma((NSUB,)),
             dma((20,)), dma((20,)), dma,
         ],
         compiler_params=pltpu.CompilerParams(
             collective_id=0, has_side_effects=True, vmem_limit_bytes=VLIM * 1024 * 1024
         ),
-    )(ref_index, ref_weights, images.reshape(ZD, NSUB, ROWS, Y))
+    )(pltpu.with_memory_space_constraint(ref_index, pltpu.HBM), pltpu.with_memory_space_constraint(ref_weights, pltpu.HBM), pltpu.with_memory_space_constraint(images.reshape(ZD, NSUB, ROWS, Y), pltpu.HBM))
     return velocity + smooth.reshape(3, 1, ZD, X, Y)
 
 

time: 54.8 us -> 52.1 us (0.951)
  local copies, waits for them, and re-layouts: 1.65 us -> 0.01 us
  Pallas kernels: 51.9 us -> 50.9 us
    unnamed x8 -> x2, local copies, waits for them, and re-layouts: 1.65 us -> 0.01 us
    pallas_call x1, Pallas kernels: 51.9 us -> 50.9 us  [on_device(): pl.pallas_call(coeff_kernel, out_shape=jax.ShapeDtypeStruct((3, ZD, X, Y)...]
where the time goes in v4:
time: 52.1 us; the launch traced here: 52 us
  Pallas kernels  50.9 us (98%)
  other arithmetic  1.07 us (2%)
    pallas_call x1, Pallas kernels, on_device(): pl.pallas_call(coeff_kernel, out_shape=jax.ShapeDtypeStruct((3, ZD, X, Y)...  50.9 us
    add x1, other arithmetic, on_device(): return velocity + smooth.reshape(3, 1, ZD, X, Y)  1.07 us

profile of v4, /device:TPU:40, one launch (start us, length us, event | category | flops | bytes accessed | tf_op | source)
XLA Modules:
  0.0 52.0 jit_solution(3538761256575860185)
XLA Ops:
  0.0 0.0 copy-start
  0.0 50.9 %shard_map.46 = f32[3,5,128,128]{3,2,1,0:T(8,128)S(1)} custom-call(s32[4]{0:T(128)} %idx_ref.1, s32[1,4]{1,0:T(1,128)} %w_ref.1, f32[5,16,8,128]{3,2,1,0:T(8,128)} %bitcast.9), custom_call_target="tpu_custom_call" | custom-call | tf_op jit(solution)/shard_map/pallas_call | solution.py:763
  50.9 0.0 copy-done
  50.9 1.1 %fusion = f32[3,1,5,128,128]{4,3,2,1,0:T(8,128)} fusion(f32[3,5,128,128]{3,2,1,0:T(8,128)S(1)} %shard_map.46, f32[3,1,5,128,128]{4,3,2,1,0:T(8,128)S(1)} %copy-done), kind=kLoop, calls=%fused_computation.1 | loop fusion | flops 245760 | bytes 2949120 | tf_op jit(solution)/shard_map/add | solution.py:795
Async XLA Ops:
  0.0 50.9 %copy-start = (f32[3,1,5,128,128]{4,3,2,1,0:T(8,128)S(1)}, f32[3,1,5,128,128]{4,3,2,1,0:T(8,128)}, u32[]{:S(2)}) copy-start(f32[3,1,5,128,128]{4,3,2,1,0:T(8,128)} %param.5) | copy-start | bytes 2949124

commit v5 on v4

--- a/solution.py
+++ b/solution.py
@@ -24,6 +24,7 @@
 NF = 2 + NREF
 FP = ZD + 2 * RG
 VLIM = 32
+ORDER = (4, 12, 8, 5, 13, 9, 6, 14, 10, 7, 15, 11, 1, 3, 2)
 MESH = pl.DeviceIdType.MESH
 
 XA, XB, ZA, ZB, CA0, CA1, CB0, CB1, IA, IB, YA, YB, FA, FB = list(range(13)) + [16]
@@ -188,7 +189,7 @@
         return remote(b_buf.at[k], b_buf.at[k], sb.at[k], rb.at[k], (s, side))
 
     def spread():
-        for k in range(1, NSUB):
+        for k in ORDER:
             chunk_out(k).start()
 
         @pl.when(cross_up)
@@ -514,13 +515,15 @@
                 for k in range(NSUB):
                     over_up(k).start()
 
+        for j, i in pairs:
+            back_out(j, i, part).start()
+
+        if part == 1:
             @pl.when(cross_lo)
             def _():
                 for k in range(NSUB):
                     over_dn(k).start()
 
-        for j, i in pairs:
-            back_out(j, i, part).start()
         base, n = parts[part]
         cf[pl.ds(RG + base, n), c] = cs[s, pl.ds(base, n)]
 
@@ -595,27 +598,7 @@
 
         lax.fori_loop(0, 3, body, 0)
 
-    def halo_part():
-        @pl.when(near_lo)
-        def _():
-            for j in range(4):
-                f_up(j).wait_recv()
-
-        @pl.when(near_up)
-        def _():
-            for j in range(4):
-                f_dn(j).wait_recv()
-
-        @pl.when(cross_up)
-        def _():
-            for k in range(NSUB):
-                over_in(k, RG + ZD, d + 1).wait_recv()
-
-        @pl.when(cross_lo)
-        def _():
-            for k in range(NSUB):
-                over_in(k, 0, d - 1).wait_recv()
-
+    def outer_part():
         matrix = band(taps, jnp.float32)
         t_high = matrix.astype(jnp.bfloat16)
         t_low = (matrix - t_high.astype(jnp.float32)).astype(jnp.bfloat16)
@@ -631,8 +614,8 @@
             high = val.astype(jnp.bfloat16)
             return high, (val - high.astype(jnp.float32)).astype(jnp.bfloat16)
 
-        def body(comp, carry):
-            for p in range(ZD):
+        def body(first, last, comp, carry):
+            for p in range(first, last):
                 total = part[comp, p] + depth_sum(comp, p, False)
                 both = jnp.dot(jnp.concatenate(split(total), axis=1), right, preferred_element_type=jnp.float32)
                 across = both[:, :Y] + both[:, Y:]
@@ -640,7 +623,29 @@
                 out[comp, p] = 40.0 * (both[:X] + both[X:])
             return carry
 
-        lax.fori_loop(0, 3, body, 0)
+        @pl.when(near_up)
+        def _():
+            for j in range(4):
+                f_dn(j).wait_recv()
+
+        @pl.when(cross_up)
+        def _():
+            for k in range(NSUB):
+                over_in(k, RG + ZD, d + 1).wait_recv()
+
+        lax.fori_loop(0, 3, functools.partial(body, RG, ZD), 0)
+
+        @pl.when(near_lo)
+        def _():
+            for j in range(4):
+                f_up(j).wait_recv()
+
+        @pl.when(cross_lo)
+        def _():
+            for k in range(NSUB):
+                over_in(k, 0, d - 1).wait_recv()
+
+        lax.fori_loop(0, 3, functools.partial(body, 0, RG), 0)
 
     def halo_drain():
         @pl.when(has_prev)
@@ -751,7 +756,7 @@
     home_end(0)
     home_end(1)
     inner_part()
-    halo_part()
+    outer_part()
     home_drain()
 
 

time: 52.1 us -> 49.8 us (0.956)
  Pallas kernels: 50.9 us -> 48.5 us
    pallas_call x1, Pallas kernels: 50.9 us -> 48.5 us  [on_device(): pl.pallas_call(coeff_kernel, out_shape=jax.ShapeDtypeStruct((3, ZD, X, Y)...]
where the time goes in v5:
time: 49.8 us; the launch traced here: 49.6 us
  Pallas kernels  48.5 us (97%)
  other arithmetic  1.07 us (2%)
    pallas_call x1, Pallas kernels, on_device(): pl.pallas_call(coeff_kernel, out_shape=jax.ShapeDtypeStruct((3, ZD, X, Y)...  48.5 us
    add x1, other arithmetic, on_device(): return velocity + smooth.reshape(3, 1, ZD, X, Y)  1.07 us

profile of v5, /device:TPU:40, one launch (start us, length us, event | category | flops | bytes accessed | tf_op | source)
XLA Modules:
  0.0 49.6 jit_solution(14317673205804161505)
XLA Ops:
  0.0 0.0 copy-start
  0.0 48.5 %shard_map.46 = f32[3,5,128,128]{3,2,1,0:T(8,128)S(1)} custom-call(s32[4]{0:T(128)} %idx_ref.1, s32[1,4]{1,0:T(1,128)} %w_ref.1, f32[5,16,8,128]{3,2,1,0:T(8,128)} %bitcast.9), custom_call_target="tpu_custom_call" | custom-call | tf_op jit(solution)/shard_map/pallas_call | solution.py:768
  48.6 0.0 copy-done
  48.6 1.1 %fusion = f32[3,1,5,128,128]{4,3,2,1,0:T(8,128)} fusion(f32[3,5,128,128]{3,2,1,0:T(8,128)S(1)} %shard_map.46, f32[3,1,5,128,128]{4,3,2,1,0:T(8,128)S(1)} %copy-done), kind=kLoop, calls=%fused_computation.1 | loop fusion | flops 245760 | bytes 2949120 | tf_op jit(solution)/shard_map/add | solution.py:800
Async XLA Ops:
  0.0 48.6 %copy-start = (f32[3,1,5,128,128]{4,3,2,1,0:T(8,128)S(1)}, f32[3,1,5,128,128]{4,3,2,1,0:T(8,128)}, u32[]{:S(2)}) copy-start(f32[3,1,5,128,128]{4,3,2,1,0:T(8,128)} %param.5) | copy-start | bytes 2949124

commit v6 on v5

--- a/solution.py
+++ b/solution.py
@@ -512,7 +512,7 @@
         if part == 0:
             @pl.when(cross_up)
             def _():
-                for k in range(NSUB):
+                for k in (8, 9, 10, 11, 7, 6, 5, 4, 12, 13, 14, 15, 0, 1, 2, 3):
                     over_up(k).start()
 
         for j, i in pairs:

time: 49.8 us -> 49.7 us (level)
  the two profiles are of different devices: /device:TPU:40 before, /device:TPU:48 now
where the time goes in v6:
time: 49.7 us; the launch traced here: 49.5 us
  Pallas kernels  48.5 us (98%)
  other arithmetic  1.07 us (2%)
    pallas_call x1, Pallas kernels, on_device(): pl.pallas_call(coeff_kernel, out_shape=jax.ShapeDtypeStruct((3, ZD, X, Y)...  48.5 us
    add x1, other arithmetic, on_device(): return velocity + smooth.reshape(3, 1, ZD, X, Y)  1.07 us

profile of v6, /device:TPU:48, one launch (start us, length us, event | category | flops | bytes accessed | tf_op | source)
XLA Modules:
  0.0 49.5 jit_solution(4159428666580261719)
XLA Ops:
  0.0 0.0 copy-start
  0.0 48.5 %shard_map.46 = f32[3,5,128,128]{3,2,1,0:T(8,128)S(1)} custom-call(s32[4]{0:T(128)} %idx_ref.1, s32[1,4]{1,0:T(1,128)} %w_ref.1, f32[5,16,8,128]{3,2,1,0:T(8,128)} %bitcast.9), custom_call_target="tpu_custom_call" | custom-call | tf_op jit(solution)/shard_map/pallas_call | solution.py:768
  48.5 0.0 copy-done
  48.5 1.1 %fusion = f32[3,1,5,128,128]{4,3,2,1,0:T(8,128)} fusion(f32[3,5,128,128]{3,2,1,0:T(8,128)S(1)} %shard_map.46, f32[3,1,5,128,128]{4,3,2,1,0:T(8,128)S(1)} %copy-done), kind=kLoop, calls=%fused_computation.1 | loop fusion | flops 245760 | bytes 2949120 | tf_op jit(solution)/shard_map/add | solution.py:800
Async XLA Ops:
  0.0 48.5 %copy-start = (f32[3,1,5,128,128]{4,3,2,1,0:T(8,128)S(1)}, f32[3,1,5,128,128]{4,3,2,1,0:T(8,128)}, u32[]{:S(2)}) copy-start(f32[3,1,5,128,128]{4,3,2,1,0:T(8,128)} %param.5) | copy-start | bytes 2949124
